TPU v7x, 256 devices: a whole 4x4x8 slice. The times are simulated.
256 devices in a mesh: ctx: 16 (over x_hi, z), head: 16 (over y, x_lo, core).
Axes of the slice: x: 4 (x_hi: 2, x_lo: 2; x = x_hi * 2 + x_lo), y: 4, z: 8, core: 2. Of those that a mesh axis runs over, the one named last changes fastest.
Arguments:
- mixer_in: bfloat16 [4096, 16384], P('ctx', 'head'), may hold values from -6 to 6
- gate_in: bfloat16 [4096, 16384], P('ctx', 'head'), may hold values from -6 to 6
- b_proj: bfloat16 [4096, 2048], P('ctx'), may hold values from -6 to 6
- c_proj: bfloat16 [4096, 2048], P('ctx'), may hold values from -0.375 to 0.375
- step_size: float32 [4096, 256], P('ctx', 'head')
- decay_log: float32 [256], P('head')
- skip_gain: float32 [256], P('head'), may hold values from 0.5 to 1.5
- entering: float32 [256, 64, 256], P('head'), may hold values from -6 to 6
- norm_gain: float32 [16384], P('head'), may hold values from 0.1 to 1.9
- w_out: bfloat16 [16384, 4096], P('head'), may hold values from -0.046875 to 0.046875
- pattern: int32 [256, 2], replicated, may hold values from 0 to 31, as said below
Outputs:
- mixed: float32 [4096, 4096], P(('ctx', 'head'))
- hessian: float32 [256, 512, 512], P(('ctx', 'head'))
Inputs may be any that keep to these rules, and one draw needn't show every extreme that they name: `pattern`: all rows differ; every pair (i, i) appears, then pairs (i, i + 1) as far as they fit in 256 rows, the other rows are further pairs drawn at random; rows in random order.
All inputs are finite; a program needn't handle non-finite values.
Results may differ from a plain program's by a relative error of at most 0.0029.
Values may be sent and summed in bfloat16 or wider, within the bound.
No kernel may reach another device: no remote copies, remote signals or barrier semaphores. Data moves between devices by JAX's collectives and lax.ppermute only.
A program may use at most 128 MiB of HBM per device.

v0:
```python
import functools

import jax
import jax.numpy as jnp
from jax import lax
from jax.experimental import pallas as pl
from jax.experimental.pallas import tpu as pltpu
from jax.sharding import Mesh, PartitionSpec as P

G = 8
N = 256
BLK = 512
HEADS = 16
PS = 64
TOK = 256
COLS = HEADS * PS
CTXN = 16
EPS = 1e-05
F32, BF16, F16 = jnp.float32, jnp.bfloat16, jnp.float16
HI = lax.Precision.HIGHEST
XB_MAX = 36.0
ENTER_MAX = 8.0
TINY = 1e-30
TOP = 14.0
LAST = 1000.0
PAY = HEADS // 2 * 16 + 8
ORDER = (4, 3, 5, 2, 6, 1, 7, 0)
VMEM = 24 * 1024 * 1024
SOURCES = 10
TILE_SCALE = 2.0**-8

CTX = ("x_hi", "z")
HEAD = ("y", "x_lo", "core")
ROWS0 = (((0,), (0,)), ((), ()))
ROWS1 = (((1,), (1,)), ((), ()))


def two(v):
    hi = v.astype(BF16)
    return hi, (v - hi.astype(F32)).astype(BF16)


def pair(w, j, lanes):
    return jnp.where(lanes < PS, w[:, 2 * j : 2 * j + 1], w[:, 2 * j + 1 : 2 * j + 2])


def exponent(bound):
    return jnp.clip(jnp.ceil(jnp.log2(jnp.maximum(bound, TINY))) + 1.0, -100.0, 127.0)


def start_kernel(g_ref, x_ref, b_ref, stept_ref, dlog_ref, pay_ref, cum_ref, cumt_ref, hi_ref, lo_ref, extra_ref):
    stept = stept_ref[...]
    own = lax.broadcasted_iota(jnp.int32, (HEADS, HEADS), 0) == lax.broadcasted_iota(jnp.int32, (HEADS, HEADS), 1)
    rate = -jnp.sum(jnp.where(own, jnp.exp(dlog_ref[...]), 0.0), axis=1, keepdims=True)
    logdt = stept * rate
    row = lax.broadcasted_iota(jnp.int32, (TOK, TOK), 0)
    col = lax.broadcasted_iota(jnp.int32, (TOK, TOK), 1)
    cum = lax.dot_general((row >= col).astype(F32), logdt, ROWS1, precision=HI, preferred_element_type=F32)
    cum_ref[...] = cum
    cumt_ref[...] = jnp.dot(logdt, (row <= col).astype(F32), precision=HI, preferred_element_type=F32)
    step = lax.dot_general((row == col).astype(F32), stept, ROWS1, precision=HI, preferred_element_type=F32)
    total = cum[TOK - 1 : TOK, :]
    w = step * jnp.exp(total - cum)
    e = exponent(XB_MAX * jnp.sum(jnp.abs(w), axis=0, keepdims=True))
    total = jnp.clip(total, -LAST, LAST)
    t0 = total.astype(BF16).astype(F32)
    t1 = (total - t0).astype(BF16).astype(F32)
    extra_ref[...] = jnp.zeros((8, 128), F32)
    for i, v in enumerate((t0, t1, total - t0 - t1, e)):
        extra_ref[i : i + 1, :HEADS] = v
    extra = extra_ref[...]
    w = w * jnp.exp2(TOP - e)
    lanes = lax.broadcasted_iota(jnp.int32, (TOK, 128), 1)
    for j in range(HEADS // 2):
        cols = slice(128 * j, 128 * j + 128)
        hi, lo = two(pair(w, j, lanes) * x_ref[:, cols].astype(F32))
        hi_ref[:, cols] = hi
        lo_ref[:, cols] = lo
    b = b_ref[...]
    state = lax.dot_general(b, hi_ref[...], ROWS0, preferred_element_type=F32) + lax.dot_general(
        b, lo_ref[...], ROWS0, preferred_element_type=F32
    )
    for c in range(CTXN):
        for j in range(HEADS // 2):
            pay_ref[c, 16 * j : 16 * j + 16, :] = state[16 * c : 16 * c + 16, 128 * j : 128 * j + 128]
        pay_ref[c, PAY - 8 :, :] = extra


def scan_kernel(at_ref, q_ref, enter_ref, out_ref):
    head = lax.broadcasted_iota(jnp.int32, (128, COLS), 0)
    spread = (lax.broadcasted_iota(jnp.int32, (128, COLS), 1) // PS == head).astype(F32)

    def wide(v):
        return jnp.dot(v, spread, precision=HI, preferred_element_type=F32)

    info = [jnp.concatenate([q_ref[c, PAY - 8 + i : PAY - 7 + i, :] for c in range(CTXN)], axis=0) for i in range(4)]
    d = jnp.exp(info[0] + info[1] + info[2])
    w = jnp.exp2(info[3])
    bounds = [jnp.full((1, 128), ENTER_MAX, F32)]
    for c in range(CTXN - 1):
        bounds.append(d[c : c + 1] * bounds[-1] + w[c : c + 1])
    e = exponent(jnp.concatenate(bounds, axis=0))
    dw, qw, ow = wide(d), wide(jnp.exp2(info[3] - TOP)), wide(jnp.exp2(TOP - e))
    rows = N // CTXN
    mine = lax.broadcasted_iota(jnp.int32, (rows, N), 0) + at_ref[1] * rows
    pick = (lax.broadcasted_iota(jnp.int32, (rows, N), 1) == mine).astype(F32)
    s = lax.dot_general(pick, enter_ref[...], ROWS1, precision=HI, preferred_element_type=F32)
    for j in range(HEADS // 2):
        cols = slice(128 * j, 128 * j + 128)
        here = slice(16 * j, 16 * j + 16)
        sj = s[:, cols]
        for c in range(CTXN):
            out_ref[c, here, :] = sj * ow[c : c + 1, cols]
            sj = dw[c : c + 1, cols] * sj + q_ref[c, here, :] * qw[c : c + 1, cols]
    for c in range(CTXN):
        out_ref[c, PAY - 8 :, :] = jnp.broadcast_to(e[c : c + 1], (8, 128))


def inner_kernel(g_ref, x_ref, b_ref, c_ref, cum_ref, cumt_ref, stept_ref, skip_ref, out_ref):
    scores = lax.dot_general(c_ref[...], b_ref[...], ROWS1, preferred_element_type=F32)
    cum = cum_ref[...]
    skip = skip_ref[...]
    half = TOK // 2
    lanes = lax.broadcasted_iota(jnp.int32, (half, 128), 1)
    for j in range(HEADS // 2):
        cols = slice(128 * j, 128 * j + 128)
        x = x_ref[:, cols]
        for r0, r1 in ((0, half), (half, TOK)):
            row = lax.broadcasted_iota(jnp.int32, (half, r1), 0) + r0
            col = lax.broadcasted_iota(jnp.int32, (half, r1), 1)
            mask = row >= col
            outs = []
            for h in (2 * j, 2 * j + 1):
                differ = cum[r0:r1, h : h + 1] - cumt_ref[h : h + 1, :r1]
                decay = jnp.where(mask, jnp.exp(jnp.where(mask, differ, 0.0)), 0.0)
                hi, lo = two(decay * scores[r0:r1, :r1] * stept_ref[h : h + 1, :r1])
                outs.append(
                    jnp.dot(hi, x[:r1], preferred_element_type=F32) + jnp.dot(lo, x[:r1], preferred_element_type=F32)
                )
            y = jnp.where(lanes < PS, outs[0], outs[1])
            out_ref[r0:r1, cols] = y + pair(skip, j, lanes[:1]) * x[r0:r1].astype(F32)


def finish_kernel(g_ref, y_ref, gate_ref, c_ref, cum_ref, gain_ref, in_ref, keep_ref, give_ref, gated_ref):
    c = c_ref[...]
    carry = jnp.exp(cum_ref[...]) * jnp.exp2(in_ref[0, PAY - 8 : PAY - 7, :HEADS] - TOP)
    half = TOK // 2
    total = jnp.zeros((TOK, 1), F32)
    lanes = lax.broadcasted_iota(jnp.int32, (TOK, 128), 1)
    for j in range(HEADS // 2):
        cols = slice(128 * j, 128 * j + 128)
        hi, lo = two(in_ref[:, 16 * j : 16 * j + 16, :].reshape(N, 128))
        inbound = jnp.dot(c, hi, preferred_element_type=F32) + jnp.dot(c, lo, preferred_element_type=F32)
        y = y_ref[:, cols] + inbound * pair(carry, j, lanes)
        g = gate_ref[:, cols].astype(F32)
        gated = y * (g / (1.0 + jnp.exp(-g)))
        gated_ref[:, cols] = gated
        total = total + jnp.sum(gated * gated, axis=1, keepdims=True)
    scale = lax.rsqrt(total / COLS + EPS)
    features = (gated_ref[...] * scale * gain_ref[...]).reshape(TOK // 32, 2, 16, COLS)
    even, odd = features[:, 0].reshape(half, COLS), features[:, 1].reshape(half, COLS)
    first = g_ref[2] == 0
    keep_ref[0] = jnp.where(first, even, odd).astype(BF16)
    give_ref[0] = jnp.where(first, odd, even).astype(BF16)


def tile_kernel(counts, where_ref, *refs):
    sources, out_refs, (held, sems) = refs[:SOURCES], refs[SOURCES:-2], refs[-2:]
    k, count = pl.program_id(0), pl.num_programs(0)
    places = [(o, x) for o in range(2) for x in range(2)]

    def copy(source, spot, column, slot, place):
        return pltpu.make_async_copy(
            source.at[spot, :, pl.ds(column, BLK)], held.at[(slot,) + place], sems.at[(slot,) + place]
        )

    def start_from(low, high, which, made):
        if high - low == 1:
            made(low).start()
            return
        middle = (low + high) // 2
        pl.when(which < middle)(lambda: start_from(low, middle, which, made))
        pl.when(which >= middle)(lambda: start_from(middle, high, which, made))

    def fetch(tile, slot):
        for n, place in enumerate(places):
            base = (tile * 4 + n) * 3
            which, spot = where_ref[base], where_ref[base + 1]
            column = pl.multiple_of(where_ref[base + 2] * BLK, BLK)
            start_from(0, SOURCES, which, lambda i: copy(sources[i], spot, column, slot, place))

    @pl.when(k == 0)
    def _():
        fetch(0, 0)

    @pl.when(k + 1 < count)
    def _():
        fetch(k + 1, (k + 1) % 2)

    slot = k % 2
    for place in places:
        copy(sources[0], 0, 0, slot, place).wait()
    a = held[slot, 0].reshape(TOK, BLK)
    b = held[slot, 1].reshape(TOK, BLK)
    tile = lax.dot_general(a, b, ROWS0, preferred_element_type=F32) * TILE_SCALE

    at = 0
    for ref, n in zip(out_refs, counts):

        @pl.when((k >= at) & (k < at + n))
        def _(ref=ref):
            ref[0] = tile

        at += n


def whole(shape):
    return pl.BlockSpec(shape, lambda *_: (0,) * len(shape))


def moved(v, axis, by):
    n = lax.axis_size(axis)
    return lax.ppermute(v, axis, [(i, (i - by) % n) for i in range(n)])


def around(v, axis):
    return [v, moved(v, axis, 1), moved(v, axis, -1), moved(v, axis, 2)]


def copy_kernel(count, pieces, *refs):
    for a, low, n, o, to in pieces:
        refs[count + o][to : to + n] = refs[a][low : low + n]


def copied(arrays, sizes, pieces):
    shape, dtype = arrays[0].shape[1:], arrays[0].dtype
    return pl.pallas_call(
        functools.partial(copy_kernel, len(arrays), pieces),
        out_shape=[jax.ShapeDtypeStruct((n,) + shape, dtype) for n in sizes],
        compiler_params=pltpu.CompilerParams(vmem_limit_bytes=VMEM),
        cost_estimate=pl.CostEstimate(flops=0, bytes_accessed=2 * sum(sizes) * 2**18, transcendentals=0),
        name="pieces",
    )(*arrays)


def across(line, axis):
    plus, minus = moved(line, axis, 1), moved(line, axis, -1)
    near, rest = copied([plus, minus], (2, 2), ((0, 0, 2, 0, 0), (1, 2, 2, 1, 0)))
    return [line, plus, minus, moved(near, axis, 1), moved(rest, axis, -1)]


def place_of(d):
    d = d % 4
    return jnp.where(d == 2, 3, jnp.where(d == 3, 2, d))


def where_found(blocks):
    head = blocks[:, :, None] // 2
    x = 2 * jnp.arange(2)[None, None, :] + head // 2 % 2
    x = place_of(x - lax.axis_index(("x_hi", "x_lo")))
    y = place_of(head // 4 - lax.axis_index("y")) + 0 * x
    other = (head % 2 != lax.axis_index("core")) + 0 * x
    outer, inner = jnp.where(other == 1, x, y), jnp.where(other == 1, y, x)
    last = (outer == 3) & (inner >= 2)
    found = (outer + last + other * 5, inner - 2 * last, blocks[:, :, None] % 2 + 0 * x)
    return jnp.stack(found, axis=-1).astype(jnp.int32).reshape(blocks.shape[0], 12)


def make_tiles(where, arrays, counts, kept):
    count, at, specs = sum(counts), 0, []
    for n in counts:
        specs.append(pl.BlockSpec((1, BLK, BLK), lambda k, w, at=at, n=n: (jnp.clip(k - at, 0, n - 1), 0, 0)))
        at += n
    return pl.pallas_call(
        functools.partial(tile_kernel, counts),
        grid_spec=pltpu.PrefetchScalarGridSpec(
            num_scalar_prefetch=1,
            grid=(count,),
            in_specs=[pl.BlockSpec(memory_space=pl.ANY)] * SOURCES,
            out_specs=specs,
            scratch_shapes=[pltpu.VMEM((2, 2, 2, TOK // 2, BLK), BF16), pltpu.SemaphoreType.DMA((2, 2, 2))],
        ),
        out_shape=[(jax.ShapeDtypeStruct if n in kept else pltpu.HBM)((counts[n], BLK, BLK), F32) for n in range(len(counts))],
        compiler_params=pltpu.CompilerParams(vmem_limit_bytes=VMEM),
        cost_estimate=pl.CostEstimate(
            flops=count * BLK**3, bytes_accessed=count * 2 * 1024 * 1024, transcendentals=0
        ),
        name="hessian_tiles",
    )(where.reshape(-1), *arrays)


def body(
    mixer_in, gate_in, b_proj, c_proj, step_size, decay_log, skip_gain, entering, norm_gain, w_out, pattern
):
    ctx_at = lax.axis_index(CTX)
    head_at = lax.axis_index(HEAD)
    place = jnp.stack([head_at * HEADS // (256 // G), ctx_at, lax.axis_index("core")]).astype(jnp.int32)
    group = pl.BlockSpec((TOK, N), lambda i, g: (0, g[0]))
    params = pltpu.CompilerParams(vmem_limit_bytes=VMEM)
    sds = jax.ShapeDtypeStruct

    stept = step_size.T
    sent, cum, cumt = pl.pallas_call(
        start_kernel,
        grid_spec=pltpu.PrefetchScalarGridSpec(
            num_scalar_prefetch=1,
            grid=(1,),
            in_specs=[whole((TOK, COLS)), group, whole((HEADS, TOK)), whole((1, HEADS))],
            out_specs=[whole((CTXN, PAY, 128)), whole((TOK, HEADS)), whole((HEADS, TOK))],
            scratch_shapes=[pltpu.VMEM((TOK, COLS), BF16)] * 2 + [pltpu.VMEM((8, 128), F32)],
        ),
        out_shape=[sds((CTXN, PAY, 128), F32), sds((TOK, HEADS), F32), sds((HEADS, TOK), F32)],
        compiler_params=params,
        name="mixer_start",
    )(place, mixer_in, b_proj, stept, decay_log[None, :])

    w_other = moved(w_out, "core", 1)
    sent = lax.all_to_all(sent.astype(F16), CTX, 0, 0, tiled=True)
    sent, w_other = lax.optimization_barrier((sent, w_other))
    sent = sent.astype(F32)
    incoming = pl.pallas_call(
        scan_kernel,
        grid_spec=pltpu.PrefetchScalarGridSpec(
            num_scalar_prefetch=1,
            grid=(1,),
            in_specs=[whole((CTXN, PAY, 128)), whole((COLS, N))],
            out_specs=whole((CTXN, PAY, 128)),
        ),
        out_shape=sds((CTXN, PAY, 128), F32),
        compiler_params=params,
        name="state_scan",
    )(place, sent, entering.reshape(COLS, N))
    incoming = lax.all_to_all(incoming.astype(F16), CTX, 0, 0, tiled=True).astype(F32)

    inner = pl.pallas_call(
        inner_kernel,
        grid_spec=pltpu.PrefetchScalarGridSpec(
            num_scalar_prefetch=1,
            grid=(1,),
            in_specs=[
                whole((TOK, COLS)), group, group, whole((TOK, HEADS)), whole((HEADS, TOK)), whole((HEADS, TOK)),
                whole((1, HEADS)),
            ],
            out_specs=whole((TOK, COLS)),
        ),
        out_shape=sds((TOK, COLS), F32),
        compiler_params=params,
        cost_estimate=pl.CostEstimate(flops=4 * TOK**3 * HEADS, bytes_accessed=2**21, transcendentals=TOK**2 * HEADS),
        name="mixer_inner",
    )(place, mixer_in, b_proj, c_proj, cum, cumt, stept, skip_gain[None, :])

    half = whole((1, TOK // 2, COLS))
    keep, give = pl.pallas_call(
        finish_kernel,
        grid_spec=pltpu.PrefetchScalarGridSpec(
            num_scalar_prefetch=1,
            grid=(1,),
            in_specs=[
                whole((TOK, COLS)), whole((TOK, COLS)), group, whole((TOK, HEADS)), whole((1, COLS)),
                whole((CTXN, PAY, 128)),
            ],
            out_specs=[half, half],
            scratch_shapes=[pltpu.VMEM((TOK, COLS), F32)],
        ),
        out_shape=[sds((1, TOK // 2, COLS), BF16)] * 2,
        compiler_params=params,
        name="mixer_finish",
    )(place, inner, gate_in, c_proj, cum, norm_gain[None, :], incoming)

    X, Y = ("x_hi", "x_lo"), "y"
    got = moved(give, "core", 1)
    lines = copied(around(keep, X) + around(got, Y), (4, 4), [(k, 0, 1, k // 4, k % 4) for k in range(8)])
    arrays = across(lines[0], Y) + across(lines[1], X)
    terms = jnp.dot(keep[0], w_out, preferred_element_type=F32) + jnp.dot(
        got[0], w_other, preferred_element_type=F32
    )
    (terms, *arrays) = lax.optimization_barrier((terms, *arrays))
    mixed = lax.psum_scatter(terms, ("y", "x_lo"), scatter_dimension=0, tiled=True)

    owned = pattern.reshape(2, 8, 8, 2, 2)[lax.axis_index("x_hi"), :, head_at // 2]
    order = jnp.array(ORDER)
    owned = owned[(lax.axis_index("z") + order) % 8]
    core = lax.axis_index("core")
    where = [where_found(owned[:, (core + k) % 2]) for k in (1, 0)]
    theirs, ours = where
    given3, own3 = make_tiles(jnp.concatenate([theirs[:3], ours[:3]]), arrays, (3, 3), (1,))
    taken3 = moved(given3, "core", 1)
    later, _ = lax.optimization_barrier((theirs[3:], given3))
    (given5,) = make_tiles(later, arrays, (5,), ())

    n = BLK // 2
    four = (own3[0] + taken3[0]).astype(F16)
    own3, taken3 = lax.optimization_barrier((own3, taken3))
    three, five = (own3[k] + taken3[k] for k in (1, 2))
    up, down = moved(four[:n], "z", -1), moved(four[n:], "z", 1)
    up, down, given5, three, five = lax.optimization_barrier((up, down, given5, three, five))
    taken5 = moved(given5, "core", 1)
    (own5,) = make_tiles(ours[3:], arrays, (5,), (0,))

    def tiles(r):
        at = ORDER.index(r) - 3
        return own5[at] + taken5[at]

    up = jnp.concatenate([up.astype(F32) + three[:n], three[n:]], axis=0).astype(F16)
    down = jnp.concatenate([five[:n], down.astype(F32) + five[n:]], axis=0).astype(F16)
    for r in (2, 1):
        up, down = moved(up, "z", -1), moved(down, "z", 1)
        up = (up.astype(F32) + tiles(r)).astype(F16)
        down = (down.astype(F32) + tiles(8 - r)).astype(F16)
    up, down = moved(up, "z", -1), moved(down, "z", 1)
    hessian = (tiles(0) + up.astype(F32) + down.astype(F32)) * (2.0 / 4096 / TILE_SCALE)
    return mixed, hessian[None]


def solution(mesh):
    fine = Mesh(mesh.devices.reshape(2, 8, 4, 2, 2), CTX + HEAD)
    in_specs = (
        P(CTX, HEAD), P(CTX, HEAD), P(CTX, None), P(CTX, None), P(CTX, HEAD), P(HEAD), P(HEAD),
        P(HEAD, None, None), P(HEAD), P(HEAD, None), P(),
    )
    out_specs = (P(CTX + HEAD, None), P(CTX + HEAD, None, None))
    return jax.shard_map(body, mesh=fine, in_specs=in_specs, out_specs=out_specs, check_vma=False)
```

profile of v0, /device:TPU:1, one launch (start us, length us, event | category | flops | bytes accessed | tf_op | source)
XLA Modules:
  0.0 238.0 jit_solution(17655256424052733853)
XLA Ops:
  7.2 3.3 %collective-permute-start = (bf16[1024,4096]{1,0:T(8,128)(2,1)}, bf16[1024,4096]{1,0:T(8,128)(2,1)}, u32[]{:S(2)}, u32[]{:S(2)}) collective-permute-start(bf16[1024,4096]{1,0:T(8,128)(2,1)} %param.21), channel_id=1, source_target_pairs={{0,1},{1,0},{2,3},{3,2},{4,5},{5,4},{6,7},{7,6},{8,9},{9,8},{10,11... | collective-permute-start | bytes 25165832 | tf_op jit(solution)/shard_map/ppermute | solution.py:223
  14.2 2.9 %mixer_start.1 = (f32[16,136,128]{2,1,0:T(8,128)S(1)}, f32[256,16]{1,0:T(8,128)S(1)}, f32[16,256]{1,0:T(8,128)S(1)}) custom-call(s32[3]{0:T(128)S(1)} %pad_add_fusion.3.g_ref.at_ref, bf16[256,1024]{1,0:T(8,128)(2,1)S(1)} %copy-done.8, bf16[256,2048]{1,0:T(8,128)(2,1)S(1)} %copy-done.5, f32[16,256]{1,0:T(8,128)S(1)} %bitcast.108, f32[1,16]{1,0:T(1,128)S(1)} %bitcast.111), custom_call_target="tpu_custom_call" | custom-call | tf_op jit(solution)/shard_map/mixer_start/pallas_call | solution.py:303
  18.1 9.1 %all-to-all-start = ((f16[16,136,128]{2,1,0:T(8,128)(2,1)}), f16[16,136,128]{2,1,0:T(8,128)(2,1)}, u32[]{:S(2)}, u32[]{:S(2)}) async-start(f16[16,136,128]{2,1,0:T(8,128)(2,1)} %convert_element_type.92), calls=%async_computation | async-start | bytes 1114112 | tf_op jit(solution)/shard_map/all_to_all | solution.py:318
  28.0 15.7 %all-to-all-done = f16[16,136,128]{2,1,0:T(8,128)(2,1)} async-done(((f16[16,136,128]{2,1,0:T(8,128)(2,1)}), f16[16,136,128]{2,1,0:T(8,128)(2,1)}, u32[]{:S(2)}, u32[]{:S(2)}) %all-to-all-start) | async-done | bytes 557088 | tf_op jit(solution)/shard_map/all_to_all | solution.py:318
  47.8 6.2 %all-to-all-start.1 = ((f16[16,136,128]{2,1,0:T(8,128)(2,1)}), f16[16,136,128]{2,1,0:T(8,128)(2,1)}, u32[]{:S(2)}, u32[]{:S(2)}) async-start(f16[16,136,128]{2,1,0:T(8,128)(2,1)} %convert_element_type.94), calls=%async_computation.1 | async-start | bytes 1114112 | tf_op jit(solution)/shard_map/all_to_all | solution.py:333
  59.5 10.4 %all-to-all-done.1 = f16[16,136,128]{2,1,0:T(8,128)(2,1)} async-done(((f16[16,136,128]{2,1,0:T(8,128)(2,1)}), f16[16,136,128]{2,1,0:T(8,128)(2,1)}, u32[]{:S(2)}, u32[]{:S(2)}) %all-to-all-start.1) | async-done | bytes 557088 | tf_op jit(solution)/shard_map/all_to_all | solution.py:333
  72.1 2.4 %mixer_finish.1 = (bf16[1,128,1024]{2,1,0:T(8,128)(2,1)S(1)}, bf16[1,128,1024]{2,1,0:T(8,128)(2,1)S(1)}) custom-call(s32[3]{0:T(128)S(1)} %pad_add_fusion.3.g_ref.at_ref, f32[256,1024]{1,0:T(8,128)S(1)} %mixer_inner.1.y_ref, bf16[256,1024]{1,0:T(8,128)(2,1)S(1)} %copy-done.7, bf16[256,2048]{1,0:T(8,128)(2,1)S(1)} %copy-done.3, ...), custom_call_target="tpu_custom_call" | custom-call | tf_op jit(solution)/shard_map/mixer_finish/pallas_call | solution.py:353
  74.5 2.8 %collective-permute-start.1 = (bf16[1,128,1024]{2,1,0:T(8,128)(2,1)S(1)}, bf16[1,128,1024]{2,1,0:T(8,128)(2,1)S(1)}, u32[]{:S(2)}, u32[]{:S(2)}) collective-permute-start(bf16[1,128,1024]{2,1,0:T(8,128)(2,1)S(1)} %get-tuple-element.41), channel_id=1, source_target_pairs={{0,1},{1,0},{2,3},{3,2},{4,5},{5,4},{6,7},{7,6},{8,9},{9,8},{10,11... | collective-permute-start | bytes 786440 | tf_op jit(solution)/shard_map/ppermute | solution.py:223
  79.7 2.7 %collective-permute-start.5 = (bf16[1,128,1024]{2,1,0:T(8,128)(2,1)S(1)}, bf16[1,128,1024]{2,1,0:T(8,128)(2,1)S(1)}, u32[]{:S(2)}, u32[]{:S(2)}) collective-permute-start(bf16[1,128,1024]{2,1,0:T(8,128)(2,1)S(1)} %collective-permute-done.1.refs_4_), channel_id=1, source_target_pairs={{0,12},{4,0},{8,4},{12,8},{1,13},{5,1},{9,5},{13,9},{2,14},{6,2},{... | collective-permute-start | bytes 786440 | tf_op jit(solution)/shard_map/ppermute | solution.py:223
  82.5 2.7 %collective-permute-done.2.refs_1_ = bf16[1,128,1024]{2,1,0:T(8,128)(2,1)S(1)} collective-permute-done((bf16[1,128,1024]{2,1,0:T(8,128)(2,1)S(1)}, bf16[1,128,1024]{2,1,0:T(8,128)(2,1)S(1)}, u32[]{:S(2)}, u32[]{:S(2)}) %collective-permute-start.2) | collective-permute-done | bytes 262176 | tf_op jit(solution)/shard_map/ppermute | solution.py:223
  85.2 2.9 %collective-permute-start.7 = (bf16[1,128,1024]{2,1,0:T(8,128)(2,1)S(1)}, bf16[1,128,1024]{2,1,0:T(8,128)(2,1)S(1)}, u32[]{:S(2)}, u32[]{:S(2)}) collective-permute-start(bf16[1,128,1024]{2,1,0:T(8,128)(2,1)S(1)} %collective-permute-done.1.refs_4_), channel_id=1, source_target_pairs={{0,8},{4,12},{8,0},{12,4},{1,9},{5,13},{9,1},{13,5},{2,10},{6,14},... | collective-permute-start | bytes 786440 | tf_op jit(solution)/shard_map/ppermute | solution.py:223
  88.1 4.2 %collective-permute-done.3.refs_2_ = bf16[1,128,1024]{2,1,0:T(8,128)(2,1)S(1)} collective-permute-done((bf16[1,128,1024]{2,1,0:T(8,128)(2,1)S(1)}, bf16[1,128,1024]{2,1,0:T(8,128)(2,1)S(1)}, u32[]{:S(2)}, u32[]{:S(2)}) %collective-permute-start.3) | collective-permute-done | bytes 262176 | tf_op jit(solution)/shard_map/ppermute | solution.py:223
  92.4 2.8 %collective-permute-done.7.refs_7_ = bf16[1,128,1024]{2,1,0:T(8,128)(2,1)S(1)} collective-permute-done((bf16[1,128,1024]{2,1,0:T(8,128)(2,1)S(1)}, bf16[1,128,1024]{2,1,0:T(8,128)(2,1)S(1)}, u32[]{:S(2)}, u32[]{:S(2)}) %collective-permute-start.7) | collective-permute-done | bytes 262176 | tf_op jit(solution)/shard_map/ppermute | solution.py:223
  101.2 4.7 %fusion.19 = f32[128,4096]{1,0:T(8,128)S(1)} fusion(bf16[1024,4096]{1,0:T(8,128)(2,1)} %param.21, bf16[1,128,1024]{2,1,0:T(8,128)(2,1)} %copy-done.2), kind=kOutput, calls=%fused_computation.37 | convolution fusion | flops 1073741824 | bytes 10747904 | tf_op jit(solution)/shard_map/dot_general | solution.py:374
  105.9 12.8 %collective-permute-done.8.refs_0_.refs_1_ = bf16[4,128,1024]{2,1,0:T(8,128)(2,1)S(1)} collective-permute-done((bf16[4,128,1024]{2,1,0:T(8,128)(2,1)}, bf16[4,128,1024]{2,1,0:T(8,128)(2,1)S(1)}, u32[]{:S(2)}, u32[]{:S(2)}) %collective-permute-start.8) | collective-permute-done | bytes 1048608 | tf_op jit(solution)/shard_map/ppermute | solution.py:223
  125.8 2.6 %collective-permute-start.14 = (bf16[2,128,1024]{2,1,0:T(8,128)(2,1)}, bf16[2,128,1024]{2,1,0:T(8,128)(2,1)}, u32[]{:S(2)}, u32[]{:S(2)}) collective-permute-start(bf16[2,128,1024]{2,1,0:T(8,128)(2,1)} %get-tuple-element.47), channel_id=1, source_target_pairs={{0,130},{2,0},{128,2},{130,128},{1,131},{3,1},{129,3},{131,129},{4... | collective-permute-start | bytes 1572872 | tf_op jit(solution)/shard_map/ppermute | solution.py:223
  128.4 6.0 %convolution_add_fusion = f32[128,4096]{1,0:T(8,128)} fusion(f32[128,4096]{1,0:T(8,128)S(1)} %fusion.19, bf16[1024,4096]{1,0:T(8,128)(2,1)} %collective-permute-done, bf16[1,128,1024]{2,1,0:T(8,128)(2,1)S(1)} %collective-permute-done.1.refs_4_), kind=kOutput, calls=%fused_computation.1 | convolution fusion | flops 1074266112 | bytes 12845056 | tf_op jit(solution)/shard_map/dot_general | solution.py:374
  136.4 3.1 %collective-permute-done.15.refs_9_ = bf16[2,128,1024]{2,1,0:T(8,128)(2,1)} collective-permute-done((bf16[2,128,1024]{2,1,0:T(8,128)(2,1)}, bf16[2,128,1024]{2,1,0:T(8,128)(2,1)}, u32[]{:S(2)}, u32[]{:S(2)}) %collective-permute-start.15) | collective-permute-done | bytes 524320 | tf_op jit(solution)/shard_map/ppermute | solution.py:223
  139.6 7.1 %hessian_tiles.4 = (f32[3,512,512]{2,1,0:T(8,128)}, f32[3,512,512]{2,1,0:T(8,128)S(1)}) custom-call(s32[72]{0:T(128)S(1)} %reshape.691.where_ref, bf16[4,128,1024]{2,1,0:T(8,128)(2,1)} %get-tuple-element.50.refs_0_, bf16[4,128,1024]{2,1,0:T(8,128)(2,1)S(1)} %collective-permute-done.8.refs_0_.refs_1_, ...), custom_call_target="tpu_custom_call" | custom-call | flops 805306368 | bytes 12582912 | tf_op jit(solution)/shard_map/hessian_tiles/pallas_call | solution.py:274
  148.3 4.5 %collective-permute-start.16 = (f32[3,512,512]{2,1,0:T(8,128)}, f32[3,512,512]{2,1,0:T(8,128)}, u32[]{:S(2)}, u32[]{:S(2)}) collective-permute-start(f32[3,512,512]{2,1,0:T(8,128)} %get-tuple-element.61), channel_id=1, source_target_pairs={{0,1},{1,0},{2,3},{3,2},{4,5},{5,4},{6,7},{7,6},{8,9},{9,8},{10,11... | collective-permute-start | bytes 9437192 | tf_op jit(solution)/shard_map/ppermute | solution.py:223
  153.2 6.7 %hessian_tiles.5 = f32[5,512,512]{2,1,0:T(8,128)} custom-call(s32[60]{0:T(128)S(1)} %reshape.692.where_ref, bf16[4,128,1024]{2,1,0:T(8,128)(2,1)} %get-tuple-element.50.refs_0_, bf16[4,128,1024]{2,1,0:T(8,128)(2,1)S(1)} %collective-permute-done.8.refs_0_.refs_1_, bf16[4,128,1024]{2,1,0:T(8,128)(2,1)S(1)} %collective-permute-done.9.refs_1_.refs_2_, ...), custom_call_target="tpu_custom_call" | custom-call | flops 671088640 | bytes 10485760 | tf_op jit(solution)/shard_map/hessian_tiles/pallas_call | solution.py:274
  164.3 3.4 %add_bitcast_fusion = (f32[512,512]{1,0:T(8,128)}, f32[512,512]{1,0:T(8,128)}) fusion(f32[3,512,512]{2,1,0:T(8,128)} %collective-permute-done.16, f32[3,512,512]{2,1,0:T(8,128)S(1)} %copy-done.1), kind=kLoop, calls=%fused_computation.26 | loop fusion | flops 524288 | bytes 6291456 | tf_op jit(solution)/shard_map/add | solution.py:394
  167.7 2.8 %collective-permute-done.17 = f16[256,512]{1,0:T(8,128)(2,1)S(1)} collective-permute-done((f16[256,512]{1,0:T(8,128)(2,1)S(1)}, f16[256,512]{1,0:T(8,128)(2,1)S(1)}, u32[]{:S(2)}, u32[]{:S(2)}) %collective-permute-start.17) | collective-permute-done | bytes 262176 | tf_op jit(solution)/shard_map/ppermute | solution.py:223
  170.5 4.6 %collective-permute-done.18 = f16[256,512]{1,0:T(8,128)(2,1)S(1)} collective-permute-done((f16[256,512]{1,0:T(8,128)(2,1)S(1)}, f16[256,512]{1,0:T(8,128)(2,1)S(1)}, u32[]{:S(2)}, u32[]{:S(2)}) %collective-permute-start.18) | collective-permute-done | bytes 262176 | tf_op jit(solution)/shard_map/ppermute | solution.py:223
  183.8 5.1 %hessian_tiles.3 = f32[5,512,512]{2,1,0:T(8,128)S(1)} custom-call(s32[60]{0:T(128)S(1)} %reshape.690.where_ref, bf16[4,128,1024]{2,1,0:T(8,128)(2,1)} %get-tuple-element.50.refs_0_, bf16[4,128,1024]{2,1,0:T(8,128)(2,1)S(1)} %collective-permute-done.8.refs_0_.refs_1_, bf16[4,128,1024]{2,1,0:T(8,128)(2,1)S(1)} %collective-permute-done.9.refs_1_.refs_2_, ...), custom_call_target="tpu_custom_call" | custom-call | flops 671088640 | bytes 10485760 | tf_op jit(solution)/shard_map/hessian_tiles/pallas_call | solution.py:274
  188.8 4.8 %collective-permute-done.20 = f16[512,512]{1,0:T(8,128)(2,1)} collective-permute-done((f16[512,512]{1,0:T(8,128)(2,1)}, f16[512,512]{1,0:T(8,128)(2,1)}, u32[]{:S(2)}, u32[]{:S(2)}) %collective-permute-start.20) | collective-permute-done | bytes 524320 | tf_op jit(solution)/shard_map/ppermute | solution.py:223
  195.8 2.5 %fusion.11 = (f16[512,512]{1,0:T(8,128)(2,1)S(1)}, f16[512,512]{1,0:T(8,128)(2,1)S(1)}) fusion(f32[5,512,512]{2,1,0:T(8,128)} %collective-permute-done.19, f32[5,512,512]{2,1,0:T(8,128)S(1)} %hessian_tiles.3, f16[512,512]{1,0:T(8,128)(2,1)} %collective-permute-done.20, f16[512,512]{1,0:T(8,128)(2,1)} %collective-permute-done.23), kind=kLoop, calls=%fused_computation.17 | loop fusion | flops 2097152 | bytes 6291456 | tf_op jit(solution)/shard_map/convert_element_type | solution.py:408
  201.0 11.0 %collective-permute-done.21 = f16[512,512]{1,0:T(8,128)(2,1)S(1)} collective-permute-done((f16[512,512]{1,0:T(8,128)(2,1)S(1)}, f16[512,512]{1,0:T(8,128)(2,1)S(1)}, u32[]{:S(2)}, u32[]{:S(2)}) %collective-permute-start.21) | collective-permute-done | bytes 524320 | tf_op jit(solution)/shard_map/ppermute | solution.py:223
  214.2 2.4 collective-permute-start.25
  216.5 9.2 %collective-permute-done.25 = f16[512,512]{1,0:T(8,128)(2,1)S(1)} collective-permute-done((f16[512,512]{1,0:T(8,128)(2,1)S(1)}, f16[512,512]{1,0:T(8,128)(2,1)S(1)}, u32[]{:S(2)}, u32[]{:S(2)}) %collective-permute-start.25) | collective-permute-done | bytes 524320 | tf_op jit(solution)/shard_map/ppermute | solution.py:223
  225.8 2.8 %collective-permute-done.22 = f16[512,512]{1,0:T(8,128)(2,1)S(1)} collective-permute-done((f16[512,512]{1,0:T(8,128)(2,1)S(1)}, f16[512,512]{1,0:T(8,128)(2,1)S(1)}, u32[]{:S(2)}, u32[]{:S(2)}) %collective-permute-start.22) | collective-permute-done | bytes 524320 | tf_op jit(solution)/shard_map/ppermute | solution.py:223
  228.6 2.6 %fusion.16 = f32[1,512,512]{2,1,0:T(8,128)} fusion(f32[5,512,512]{2,1,0:T(8,128)} %collective-permute-done.19, f32[5,512,512]{2,1,0:T(8,128)S(1)} %hessian_tiles.3, f16[512,512]{1,0:T(8,128)(2,1)S(1)} %collective-permute-done.25, f16[512,512]{1,0:T(8,128)(2,1)S(1)} %collective-permute-done.22), kind=kLoop, calls=%fused_computation.23 | loop fusion | flops 1572864 | bytes 4194304 | tf_op jit(solution)/shard_map/broadcast_in_dim | solution.py:412
  (121 shorter events, 56.8 us)
Async XLA Ops:
  7.2 36.5 %collective-permute-start = (bf16[1024,4096]{1,0:T(8,128)(2,1)}, bf16[1024,4096]{1,0:T(8,128)(2,1)}, u32[]{:S(2)}, u32[]{:S(2)}) collective-permute-start(bf16[1024,4096]{1,0:T(8,128)(2,1)} %param.21), channel_id=1, source_target_pairs={{0,1},{1,0},{2,3},{3,2},{4,5},{5,4},{6,7},{7,6},{8,9},{9,8},{10,11... | collective-permute-start | bytes 25165832 | tf_op jit(solution)/shard_map/ppermute | solution.py:223
  17.2 37.9 %copy-start.3 = (bf16[256,2048]{1,0:T(8,128)(2,1)S(1)}, bf16[256,2048]{1,0:T(8,128)(2,1)}, u32[]{:S(2)}) copy-start(bf16[256,2048]{1,0:T(8,128)(2,1)} %c_ref.3) | copy-start | bytes 3145732
  17.2 37.9 %copy-start.6 = (bf16[256,2048]{1,0:T(8,128)(2,1)S(1)}, bf16[256,2048]{1,0:T(8,128)(2,1)}, u32[]{:S(2)}) copy-start(bf16[256,2048]{1,0:T(8,128)(2,1)} %b_ref.3) | copy-start | bytes 3145732
  17.2 37.9 %copy-start.11 = (f32[256,16]{0,1:T(8,128)S(1)}, f32[256,16]{0,1:T(8,128)}, u32[]{:S(2)}) copy-start(f32[256,16]{0,1:T(8,128)} %param.16) | copy-start | bytes 49156
  18.1 25.6 %all-to-all-start = ((f16[16,136,128]{2,1,0:T(8,128)(2,1)}), f16[16,136,128]{2,1,0:T(8,128)(2,1)}, u32[]{:S(2)}, u32[]{:S(2)}) async-start(f16[16,136,128]{2,1,0:T(8,128)(2,1)} %convert_element_type.92), calls=%async_computation | async-start | bytes 1114112 | tf_op jit(solution)/shard_map/all_to_all | solution.py:318
  47.8 22.1 %all-to-all-start.1 = ((f16[16,136,128]{2,1,0:T(8,128)(2,1)}), f16[16,136,128]{2,1,0:T(8,128)(2,1)}, u32[]{:S(2)}, u32[]{:S(2)}) async-start(f16[16,136,128]{2,1,0:T(8,128)(2,1)} %convert_element_type.94), calls=%async_computation.1 | async-start | bytes 1114112 | tf_op jit(solution)/shard_map/all_to_all | solution.py:333
  54.0 177.2 %reduce-scatter.2.cloned.1.call-start = ((), (), s32[]{:S(2)}) async-start(), calls=%async_computation.3 | async-start | bytes 2359296 | tf_op jit(solution)/shard_map/reduce_scatter | solution.py:378
  74.5 5.2 %collective-permute-start.1 = (bf16[1,128,1024]{2,1,0:T(8,128)(2,1)S(1)}, bf16[1,128,1024]{2,1,0:T(8,128)(2,1)S(1)}, u32[]{:S(2)}, u32[]{:S(2)}) collective-permute-start(bf16[1,128,1024]{2,1,0:T(8,128)(2,1)S(1)} %get-tuple-element.41), channel_id=1, source_target_pairs={{0,1},{1,0},{2,3},{3,2},{4,5},{5,4},{6,7},{7,6},{8,9},{9,8},{10,11... | collective-permute-start | bytes 786440 | tf_op jit(solution)/shard_map/ppermute | solution.py:223
  77.3 7.9 %collective-permute-start.2 = (bf16[1,128,1024]{2,1,0:T(8,128)(2,1)S(1)}, bf16[1,128,1024]{2,1,0:T(8,128)(2,1)S(1)}, u32[]{:S(2)}, u32[]{:S(2)}) collective-permute-start(bf16[1,128,1024]{2,1,0:T(8,128)(2,1)S(1)} %get-tuple-element.40.refs_0_), channel_id=1, source_target_pairs={{0,130},{2,0},{128,2},{130,128},{1,131},{3,1},{129,3},{131,129},{4... | collective-permute-start | bytes 786440 | tf_op jit(solution)/shard_map/ppermute | solution.py:223
  77.9 14.4 %collective-permute-start.3 = (bf16[1,128,1024]{2,1,0:T(8,128)(2,1)S(1)}, bf16[1,128,1024]{2,1,0:T(8,128)(2,1)S(1)}, u32[]{:S(2)}, u32[]{:S(2)}) collective-permute-start(bf16[1,128,1024]{2,1,0:T(8,128)(2,1)S(1)} %get-tuple-element.40.refs_0_), channel_id=1, source_target_pairs={{0,2},{2,128},{128,130},{130,0},{1,3},{3,129},{129,131},{131,1},{4... | collective-permute-start | bytes 786440 | tf_op jit(solution)/shard_map/ppermute | solution.py:223
  78.9 13.5 %collective-permute-start.4 = (bf16[1,128,1024]{2,1,0:T(8,128)(2,1)S(1)}, bf16[1,128,1024]{2,1,0:T(8,128)(2,1)S(1)}, u32[]{:S(2)}, u32[]{:S(2)}) collective-permute-start(bf16[1,128,1024]{2,1,0:T(8,128)(2,1)S(1)} %get-tuple-element.40.refs_0_), channel_id=1, source_target_pairs={{0,128},{2,130},{128,0},{130,2},{1,129},{3,131},{129,1},{131,3},{4... | collective-permute-start | bytes 786440 | tf_op jit(solution)/shard_map/ppermute | solution.py:223
  79.7 12.6 %collective-permute-start.5 = (bf16[1,128,1024]{2,1,0:T(8,128)(2,1)S(1)}, bf16[1,128,1024]{2,1,0:T(8,128)(2,1)S(1)}, u32[]{:S(2)}, u32[]{:S(2)}) collective-permute-start(bf16[1,128,1024]{2,1,0:T(8,128)(2,1)S(1)} %collective-permute-done.1.refs_4_), channel_id=1, source_target_pairs={{0,12},{4,0},{8,4},{12,8},{1,13},{5,1},{9,5},{13,9},{2,14},{6,2},{... | collective-permute-start | bytes 786440 | tf_op jit(solution)/shard_map/ppermute | solution.py:223
  82.5 9.9 %collective-permute-start.6 = (bf16[1,128,1024]{2,1,0:T(8,128)(2,1)S(1)}, bf16[1,128,1024]{2,1,0:T(8,128)(2,1)S(1)}, u32[]{:S(2)}, u32[]{:S(2)}) collective-permute-start(bf16[1,128,1024]{2,1,0:T(8,128)(2,1)S(1)} %collective-permute-done.1.refs_4_), channel_id=1, source_target_pairs={{0,4},{4,8},{8,12},{12,0},{1,5},{5,9},{9,13},{13,1},{2,6},{6,10},{... | collective-permute-start | bytes 786440 | tf_op jit(solution)/shard_map/ppermute | solution.py:223
  85.2 9.9 %collective-permute-start.7 = (bf16[1,128,1024]{2,1,0:T(8,128)(2,1)S(1)}, bf16[1,128,1024]{2,1,0:T(8,128)(2,1)S(1)}, u32[]{:S(2)}, u32[]{:S(2)}) collective-permute-start(bf16[1,128,1024]{2,1,0:T(8,128)(2,1)S(1)} %collective-permute-done.1.refs_4_), channel_id=1, source_target_pairs={{0,8},{4,12},{8,0},{12,4},{1,9},{5,13},{9,1},{13,5},{2,10},{6,14},... | collective-permute-start | bytes 786440 | tf_op jit(solution)/shard_map/ppermute | solution.py:223
  96.6 22.1 %collective-permute-start.8 = (bf16[4,128,1024]{2,1,0:T(8,128)(2,1)}, bf16[4,128,1024]{2,1,0:T(8,128)(2,1)S(1)}, u32[]{:S(2)}, u32[]{:S(2)}) collective-permute-start(bf16[4,128,1024]{2,1,0:T(8,128)(2,1)} %get-tuple-element.50.refs_0_), channel_id=1, source_target_pairs={{0,12},{4,0},{8,4},{12,8},{1,13},{5,1},{9,5},{13,9},{2,14},{6,2},{... | collective-permute-start | bytes 3145736 | tf_op jit(solution)/shard_map/ppermute | solution.py:223
  97.4 23.6 %collective-permute-start.9 = (bf16[4,128,1024]{2,1,0:T(8,128)(2,1)}, bf16[4,128,1024]{2,1,0:T(8,128)(2,1)S(1)}, u32[]{:S(2)}, u32[]{:S(2)}) collective-permute-start(bf16[4,128,1024]{2,1,0:T(8,128)(2,1)} %get-tuple-element.50.refs_0_), channel_id=1, source_target_pairs={{0,4},{4,8},{8,12},{12,0},{1,5},{5,9},{9,13},{13,1},{2,6},{6,10},{... | collective-permute-start | bytes 3145736 | tf_op jit(solution)/shard_map/ppermute | solution.py:223
  98.1 25.5 %collective-permute-start.12 = (bf16[4,128,1024]{2,1,0:T(8,128)(2,1)}, bf16[4,128,1024]{2,1,0:T(8,128)(2,1)S(1)}, u32[]{:S(2)}, u32[]{:S(2)}) collective-permute-start(bf16[4,128,1024]{2,1,0:T(8,128)(2,1)} %get-tuple-element.55.refs_5_), channel_id=1, source_target_pairs={{0,130},{2,0},{128,2},{130,128},{1,131},{3,1},{129,3},{131,129},{4... | collective-permute-start | bytes 3145736 | tf_op jit(solution)/shard_map/ppermute | solution.py:223
  99.9 23.7 %collective-permute-start.13 = (bf16[4,128,1024]{2,1,0:T(8,128)(2,1)}, bf16[4,128,1024]{2,1,0:T(8,128)(2,1)}, u32[]{:S(2)}, u32[]{:S(2)}) collective-permute-start(bf16[4,128,1024]{2,1,0:T(8,128)(2,1)} %get-tuple-element.55.refs_5_), channel_id=1, source_target_pairs={{0,2},{2,128},{128,130},{130,0},{1,3},{3,129},{129,131},{131,1},{4... | collective-permute-start | bytes 3145736 | tf_op jit(solution)/shard_map/ppermute | solution.py:223
  122.1 12.3 %collective-permute-start.10 = (bf16[2,128,1024]{2,1,0:T(8,128)(2,1)}, bf16[2,128,1024]{2,1,0:T(8,128)(2,1)}, u32[]{:S(2)}, u32[]{:S(2)}) collective-permute-start(bf16[2,128,1024]{2,1,0:T(8,128)(2,1)} %get-tuple-element.44), channel_id=1, source_target_pairs={{0,12},{4,0},{8,4},{12,8},{1,13},{5,1},{9,5},{13,9},{2,14},{6,2},{... | collective-permute-start | bytes 1572872 | tf_op jit(solution)/shard_map/ppermute | solution.py:223
  122.4 12.0 %collective-permute-start.11 = (bf16[2,128,1024]{2,1,0:T(8,128)(2,1)}, bf16[2,128,1024]{2,1,0:T(8,128)(2,1)}, u32[]{:S(2)}, u32[]{:S(2)}) collective-permute-start(bf16[2,128,1024]{2,1,0:T(8,128)(2,1)} %get-tuple-element.45), channel_id=1, source_target_pairs={{0,4},{4,8},{8,12},{12,0},{1,5},{5,9},{9,13},{13,1},{2,6},{6,10},{... | collective-permute-start | bytes 1572872 | tf_op jit(solution)/shard_map/ppermute | solution.py:223
  125.8 10.6 %collective-permute-start.14 = (bf16[2,128,1024]{2,1,0:T(8,128)(2,1)}, bf16[2,128,1024]{2,1,0:T(8,128)(2,1)}, u32[]{:S(2)}, u32[]{:S(2)}) collective-permute-start(bf16[2,128,1024]{2,1,0:T(8,128)(2,1)} %get-tuple-element.47), channel_id=1, source_target_pairs={{0,130},{2,0},{128,2},{130,128},{1,131},{3,1},{129,3},{131,129},{4... | collective-permute-start | bytes 1572872 | tf_op jit(solution)/shard_map/ppermute | solution.py:223
  128.4 11.1 %collective-permute-start.15 = (bf16[2,128,1024]{2,1,0:T(8,128)(2,1)}, bf16[2,128,1024]{2,1,0:T(8,128)(2,1)}, u32[]{:S(2)}, u32[]{:S(2)}) collective-permute-start(bf16[2,128,1024]{2,1,0:T(8,128)(2,1)} %get-tuple-element.48), channel_id=1, source_target_pairs={{0,2},{2,128},{128,130},{130,0},{1,3},{3,129},{129,131},{131,1},{4... | collective-permute-start | bytes 1572872 | tf_op jit(solution)/shard_map/ppermute | solution.py:223
  148.3 11.6 %collective-permute-start.16 = (f32[3,512,512]{2,1,0:T(8,128)}, f32[3,512,512]{2,1,0:T(8,128)}, u32[]{:S(2)}, u32[]{:S(2)}) collective-permute-start(f32[3,512,512]{2,1,0:T(8,128)} %get-tuple-element.61), channel_id=1, source_target_pairs={{0,1},{1,0},{2,3},{3,2},{4,5},{5,4},{6,7},{7,6},{8,9},{9,8},{10,11... | collective-permute-start | bytes 9437192 | tf_op jit(solution)/shard_map/ppermute | solution.py:223
  161.6 9.0 %collective-permute-start.17 = (f16[256,512]{1,0:T(8,128)(2,1)S(1)}, f16[256,512]{1,0:T(8,128)(2,1)S(1)}, u32[]{:S(2)}, u32[]{:S(2)}) collective-permute-start(f16[256,512]{1,0:T(8,128)(2,1)S(1)} %get-tuple-element.87), channel_id=1, source_target_pairs={{0,16},{16,32},{32,48},{48,64},{64,80},{80,96},{96,112},{112,0},{1... | collective-permute-start | bytes 786440 | tf_op jit(solution)/shard_map/ppermute | solution.py:223
  163.3 11.8 %collective-permute-start.18 = (f16[256,512]{1,0:T(8,128)(2,1)S(1)}, f16[256,512]{1,0:T(8,128)(2,1)S(1)}, u32[]{:S(2)}, u32[]{:S(2)}) collective-permute-start(f16[256,512]{1,0:T(8,128)(2,1)S(1)} %get-tuple-element.86), channel_id=1, source_target_pairs={{0,112},{16,0},{32,16},{48,32},{64,48},{80,64},{96,80},{112,96},{1... | collective-permute-start | bytes 786440 | tf_op jit(solution)/shard_map/ppermute | solution.py:223
  175.2 20.6 %collective-permute-start.19 = (f32[5,512,512]{2,1,0:T(8,128)}, f32[5,512,512]{2,1,0:T(8,128)}, u32[]{:S(2)}, u32[]{:S(2)}) collective-permute-start(f32[5,512,512]{2,1,0:T(8,128)} %hessian_tiles.5), channel_id=1, source_target_pairs={{0,1},{1,0},{2,3},{3,2},{4,5},{5,4},{6,7},{7,6},{8,9},{9,8},{10,11... | collective-permute-start | bytes 15728648 | tf_op jit(solution)/shard_map/ppermute | solution.py:223
  178.5 15.1 %collective-permute-start.20 = (f16[512,512]{1,0:T(8,128)(2,1)}, f16[512,512]{1,0:T(8,128)(2,1)}, u32[]{:S(2)}, u32[]{:S(2)}) collective-permute-start(f16[512,512]{1,0:T(8,128)(2,1)} %pad_maximum_fusion), channel_id=1, source_target_pairs={{0,16},{16,32},{32,48},{48,64},{64,80},{80,96},{96,112},{112,0},{1... | collective-permute-start | bytes 1572872 | tf_op jit(solution)/shard_map/ppermute | solution.py:223
  182.2 13.6 %collective-permute-start.23 = (f16[512,512]{1,0:T(8,128)(2,1)}, f16[512,512]{1,0:T(8,128)(2,1)}, u32[]{:S(2)}, u32[]{:S(2)}) collective-permute-start(f16[512,512]{1,0:T(8,128)(2,1)} %pad_maximum_fusion.1), channel_id=1, source_target_pairs={{0,112},{16,0},{32,16},{48,32},{64,48},{80,64},{96,80},{112,96},{1... | collective-permute-start | bytes 1572872 | tf_op jit(solution)/shard_map/ppermute | solution.py:223
  198.3 13.7 %collective-permute-start.21 = (f16[512,512]{1,0:T(8,128)(2,1)S(1)}, f16[512,512]{1,0:T(8,128)(2,1)S(1)}, u32[]{:S(2)}, u32[]{:S(2)}) collective-permute-start(f16[512,512]{1,0:T(8,128)(2,1)S(1)} %get-tuple-element.78), channel_id=1, source_target_pairs={{0,16},{16,32},{32,48},{48,64},{64,80},{80,96},{96,112},{112,0},{1... | collective-permute-start | bytes 1572872 | tf_op jit(solution)/shard_map/ppermute | solution.py:223
  199.1 12.9 %collective-permute-start.24 = (f16[512,512]{1,0:T(8,128)(2,1)S(1)}, f16[512,512]{1,0:T(8,128)(2,1)S(1)}, u32[]{:S(2)}, u32[]{:S(2)}) collective-permute-start(f16[512,512]{1,0:T(8,128)(2,1)S(1)} %get-tuple-element.79), channel_id=1, source_target_pairs={{0,112},{16,0},{32,16},{48,32},{64,48},{80,64},{96,80},{112,96},{1... | collective-permute-start | bytes 1572872 | tf_op jit(solution)/shard_map/ppermute | solution.py:223
  214.2 11.6 %collective-permute-start.25 = (f16[512,512]{1,0:T(8,128)(2,1)S(1)}, f16[512,512]{1,0:T(8,128)(2,1)S(1)}, u32[]{:S(2)}, u32[]{:S(2)}) collective-permute-start(f16[512,512]{1,0:T(8,128)(2,1)S(1)} %get-tuple-element.77), channel_id=1, source_target_pairs={{0,112},{16,0},{32,16},{48,32},{64,48},{80,64},{96,80},{112,96},{1... | collective-permute-start | bytes 1572872 | tf_op jit(solution)/shard_map/ppermute | solution.py:223
  216.5 12.0 %collective-permute-start.22 = (f16[512,512]{1,0:T(8,128)(2,1)S(1)}, f16[512,512]{1,0:T(8,128)(2,1)S(1)}, u32[]{:S(2)}, u32[]{:S(2)}) collective-permute-start(f16[512,512]{1,0:T(8,128)(2,1)S(1)} %get-tuple-element.76), channel_id=1, source_target_pairs={{0,16},{16,32},{32,48},{48,64},{64,80},{80,96},{96,112},{112,0},{1... | collective-permute-start | bytes 1572872 | tf_op jit(solution)/shard_map/ppermute | solution.py:223
  (14 other events, 179.7 us)
Sparse Core Ops, SparseCore 0:
  176.3 49.1 reduce-scatter.1
where the time goes:
time: 241 us; the launch traced here: 238 us
  waiting for transfers between devices  93.5 us (39%)
  starting transfers between devices  52.8 us (22%)
  Pallas kernels  33.3 us (14%)
  other arithmetic  22.9 us (10%)
  between operations  14.4 us (6%)
  matrix products  10.7 us (4%)
  local copies, waits for them, and re-layouts  10.4 us (4%)
    ppermute x26, waiting for transfers between devices, moved(): return lax.ppermute(v, axis, [(i, (i - by) % n) for i in range(n)])  67.4 us
    ppermute x26, starting transfers between devices, moved(): return lax.ppermute(v, axis, [(i, (i - by) % n) for i in range(n)])  37.5 us
    pallas_call x3, Pallas kernels, make_tiles(): pl.pallas_call(functools.partial(tile_kernel, counts), grid_spec=pltpu.Pr...  18.9 us
    all_to_all x1, waiting for transfers between devices, body(): sent = lax.all_to_all(sent.astype(F16), CTX, 0, 0, tiled=True)  15.7 us
    all_to_all x1, waiting for transfers between devices, body(): lax.all_to_all(incoming.astype(F16), CTX, 0, 0, tiled=True).astype(F32)  10.4 us
    all_to_all x1, starting transfers between devices, body(): sent = lax.all_to_all(sent.astype(F16), CTX, 0, 0, tiled=True)  9.06 us
    unnamed x34, local copies, waits for them, and re-layouts  7.44 us
    all_to_all x1, starting transfers between devices, body(): lax.all_to_all(incoming.astype(F16), CTX, 0, 0, tiled=True).astype(F32)  6.16 us
  transfers between devices with their start and end apart: 29, of which 16 were waited for; matrix products, arithmetic and copies ran while one was open for 13% of the time, Pallas kernels for 8%

commit v1 on v0

--- a/solution.py
+++ b/solution.py
@@ -224,7 +224,8 @@
 
 
 def around(v, axis):
-    return [v, moved(v, axis, 1), moved(v, axis, -1), moved(v, axis, 2)]
+    far = moved(v, axis, 2)
+    return [v, moved(v, axis, 1), moved(v, axis, -1), far]
 
 
 def copy_kernel(count, pieces, *refs):
@@ -383,26 +384,33 @@
     core = lax.axis_index("core")
     where = [where_found(owned[:, (core + k) % 2]) for k in (1, 0)]
     theirs, ours = where
-    given3, own3 = make_tiles(jnp.concatenate([theirs[:3], ours[:3]]), arrays, (3, 3), (1,))
+    (given3,) = make_tiles(theirs[:3], arrays, (3,), ())
+    later, given3 = lax.optimization_barrier((ours[:3], given3))
     taken3 = moved(given3, "core", 1)
-    later, _ = lax.optimization_barrier((theirs[3:], given3))
+    (own3,) = make_tiles(later, arrays, (3,), ())
+    four = (own3[0] + taken3[0]).astype(F16)
+    four, own3, taken3 = lax.optimization_barrier((four, own3, taken3))
+
+    n = BLK // 2
+    up, down = moved(four[:n], "z", -1), moved(four[n:], "z", 1)
+    three, five = (own3[k] + taken3[k] for k in (1, 2))
+    beside = (three.astype(F16), five.astype(F16))
+    later, beside = lax.optimization_barrier((theirs[3:], beside))
     (given5,) = make_tiles(later, arrays, (5,), ())
-
-    n = BLK // 2
-    four = (own3[0] + taken3[0]).astype(F16)
-    own3, taken3 = lax.optimization_barrier((own3, taken3))
-    three, five = (own3[k] + taken3[k] for k in (1, 2))
-    up, down = moved(four[:n], "z", -1), moved(four[n:], "z", 1)
-    up, down, given5, three, five = lax.optimization_barrier((up, down, given5, three, five))
+    up, down, given5, beside = lax.optimization_barrier((up, down, given5, beside))
     taken5 = moved(given5, "core", 1)
     (own5,) = make_tiles(ours[3:], arrays, (5,), (0,))
+    two_ways = [(own5, taken5), lax.optimization_barrier((own5, taken5))]
 
     def tiles(r):
         at = ORDER.index(r) - 3
-        return own5[at] + taken5[at]
-
-    up = jnp.concatenate([up.astype(F32) + three[:n], three[n:]], axis=0).astype(F16)
-    down = jnp.concatenate([five[:n], down.astype(F32) + five[n:]], axis=0).astype(F16)
+        own, taken = two_ways[r > 4]
+        return own[at] + taken[at]
+
+    up = up.astype(F32) + own3[1, :n] + taken3[1, :n]
+    down = down.astype(F32) + own3[2, n:] + taken3[2, n:]
+    up = lax.dynamic_update_slice(beside[0], up.astype(F16), (0, 0))
+    down = lax.dynamic_update_slice(beside[1], down.astype(F16), (n, 0))
     for r in (2, 1):
         up, down = moved(up, "z", -1), moved(down, "z", 1)
         up = (up.astype(F32) + tiles(r)).astype(F16)

time: 241 us -> 230 us (0.954)
  waiting for transfers between devices: 93.5 us -> 64.6 us
  blocking collectives: 0 us -> 28 us
  starting transfers between devices: 52.8 us -> 42.5 us
  Pallas kernels: 33.3 us -> 37 us
    all_to_all x0 -> x1, blocking collectives: none -> 28 us  [body(): sent = lax.all_to_all(sent.astype(F16), CTX, 0, 0, tiled=True)]
    all_to_all x1 -> x0, waiting for transfers between devices: 15.7 us -> none  [body(): sent = lax.all_to_all(sent.astype(F16), CTX, 0, 0, tiled=True)]
    ppermute x26, waiting for transfers between devices: 67.4 us -> 54.5 us  [moved(): return lax.ppermute(v, axis, [(i, (i - by) % n) for i in range(n)])]
    all_to_all x1 -> x0, starting transfers between devices: 9.06 us -> none  [body(): sent = lax.all_to_all(sent.astype(F16), CTX, 0, 0, tiled=True)]
    convert_element_type x0 -> x3, other arithmetic: none -> 6.92 us  [the longest x1 3.68 us: body(): beside = (three.astype(F16), five.astype(F16))]
    pallas_call x3 -> x4, Pallas kernels: 18.9 us -> 22.6 us  [make_tiles(): pl.pallas_call(functools.partial(tile_kernel, counts), grid_spec=pltpu.Pr...]
    add x1 -> x0, other arithmetic: 3.44 us -> none  [body(): three, five = (own3[k] + taken3[k] for k in (1, 2))]
    another operation x2 -> x0, other arithmetic: 2.72 us -> none
  transfers between devices with their start and end apart: 29 -> 28, of which waited for: 16 -> 14; matrix products, arithmetic and copies ran while one was open for 13% -> 13% of each run, Pallas kernels for 8% -> 11%
where the time goes in v1:
time: 230 us; the launch traced here: 227 us
  waiting for transfers between devices  64.6 us (28%)
  starting transfers between devices  42.5 us (18%)
  Pallas kernels  37 us (16%)
  blocking collectives  28 us (12%)
  other arithmetic  20.9 us (9%)
  between operations  14.5 us (6%)
  matrix products  10.8 us (5%)
  local copies, waits for them, and re-layouts  8.81 us (4%)
    ppermute x26, waiting for transfers between devices, moved(): return lax.ppermute(v, axis, [(i, (i - by) % n) for i in range(n)])  54.5 us
    ppermute x26, starting transfers between devices, moved(): return lax.ppermute(v, axis, [(i, (i - by) % n) for i in range(n)])  38.2 us
    all_to_all x1, blocking collectives, body(): sent = lax.all_to_all(sent.astype(F16), CTX, 0, 0, tiled=True)  28 us
    pallas_call x4, Pallas kernels, make_tiles(): pl.pallas_call(functools.partial(tile_kernel, counts), grid_spec=pltpu.Pr...  22.6 us
    all_to_all x1, waiting for transfers between devices, body(): lax.all_to_all(incoming.astype(F16), CTX, 0, 0, tiled=True).astype(F32)  9.65 us
    dot_general x1, matrix products, body(): jnp.dot(got[0], w_other, preferred_element_type=F32)  6.02 us
    unnamed x30, local copies, waits for them, and re-layouts  5.77 us
    dot_general x1, matrix products, body(): jnp.dot(keep[0], w_out, preferred_element_type=F32)  4.74 us
  transfers between devices with their start and end apart: 28, of which 14 were waited for; matrix products, arithmetic and copies ran while one was open for 13% of the time, Pallas kernels for 11%

profile of v1, /device:TPU:1, one launch (start us, length us, event | category | flops | bytes accessed | tf_op | source)
XLA Modules:
  0.0 227.0 jit_solution(1249455209167807177)
XLA Ops:
  7.2 3.3 %collective-permute-start = (bf16[1024,4096]{1,0:T(8,128)(2,1)}, bf16[1024,4096]{1,0:T(8,128)(2,1)}, u32[]{:S(2)}, u32[]{:S(2)}) collective-permute-start(bf16[1024,4096]{1,0:T(8,128)(2,1)} %param.21), channel_id=1, source_target_pairs={{0,1},{1,0},{2,3},{3,2},{4,5},{5,4},{6,7},{7,6},{8,9},{9,8},{10,11... | collective-permute-start | bytes 25165832 | tf_op jit(solution)/shard_map/ppermute | solution.py:223
  14.2 2.9 %mixer_start.1 = (f32[16,136,128]{2,1,0:T(8,128)S(1)}, f32[256,16]{1,0:T(8,128)S(1)}, f32[16,256]{1,0:T(8,128)S(1)}) custom-call(s32[3]{0:T(128)S(1)} %pad_add_fusion.2.g_ref.at_ref, bf16[256,1024]{1,0:T(8,128)(2,1)S(1)} %copy-done.6, bf16[256,2048]{1,0:T(8,128)(2,1)S(1)} %copy-done.3, f32[16,256]{1,0:T(8,128)S(1)} %bitcast.126, f32[1,16]{1,0:T(1,128)S(1)} %bitcast.129), custom_call_target="tpu_custom_call" | custom-call | tf_op jit(solution)/shard_map/mixer_start/pallas_call | solution.py:304
  17.3 28.0 %all_to_all.10 = f16[16,136,128]{2,1,0:T(8,128)(2,1)S(1)} all-to-all(f16[16,136,128]{2,1,0:T(8,128)(2,1)S(1)} %convert_element_type.110), channel_id=1, replica_groups=mesh['x_hi'=2,'z'=8,'y'=4,'x_lo'=2,'core'=2] {'x_hi','z'}, dimensions={0} | all-to-all | bytes 1114112 | tf_op jit(solution)/shard_map/all_to_all | solution.py:319
  48.3 4.3 %all-to-all-start.1 = ((f16[16,136,128]{2,1,0:T(8,128)(2,1)}), f16[16,136,128]{2,1,0:T(8,128)(2,1)}, u32[]{:S(2)}, u32[]{:S(2)}) async-start(f16[16,136,128]{2,1,0:T(8,128)(2,1)} %convert_element_type.112), calls=%async_computation.1 | async-start | bytes 1114112 | tf_op jit(solution)/shard_map/all_to_all | solution.py:334
  54.9 2.3 mixer_inner.1.y_ref
  57.7 9.7 %all-to-all-done.1 = f16[16,136,128]{2,1,0:T(8,128)(2,1)} async-done(((f16[16,136,128]{2,1,0:T(8,128)(2,1)}), f16[16,136,128]{2,1,0:T(8,128)(2,1)}, u32[]{:S(2)}, u32[]{:S(2)}) %all-to-all-start.1) | async-done | bytes 557088 | tf_op jit(solution)/shard_map/all_to_all | solution.py:334
  69.6 2.4 %mixer_finish.1 = (bf16[1,128,1024]{2,1,0:T(8,128)(2,1)S(1)}, bf16[1,128,1024]{2,1,0:T(8,128)(2,1)S(1)}) custom-call(s32[3]{0:T(128)S(1)} %pad_add_fusion.2.g_ref.at_ref, f32[256,1024]{1,0:T(8,128)S(1)} %mixer_inner.1.y_ref, bf16[256,1024]{1,0:T(8,128)(2,1)S(1)} %copy-done.5, bf16[256,2048]{1,0:T(8,128)(2,1)S(1)} %copy-done.1, ...), custom_call_target="tpu_custom_call" | custom-call | tf_op jit(solution)/shard_map/mixer_finish/pallas_call | solution.py:354
  72.0 3.5 %collective-permute-start.1 = (bf16[1,128,1024]{2,1,0:T(8,128)(2,1)S(1)}, bf16[1,128,1024]{2,1,0:T(8,128)(2,1)S(1)}, u32[]{:S(2)}, u32[]{:S(2)}) collective-permute-start(bf16[1,128,1024]{2,1,0:T(8,128)(2,1)S(1)} %get-tuple-element.46), channel_id=1, source_target_pairs={{0,1},{1,0},{2,3},{3,2},{4,5},{5,4},{6,7},{7,6},{8,9},{9,8},{10,11... | collective-permute-start | bytes 786440 | tf_op jit(solution)/shard_map/ppermute | solution.py:223
  78.1 2.8 %collective-permute-start.5 = (bf16[1,128,1024]{2,1,0:T(8,128)(2,1)S(1)}, bf16[1,128,1024]{2,1,0:T(8,128)(2,1)S(1)}, u32[]{:S(2)}, u32[]{:S(2)}) collective-permute-start(bf16[1,128,1024]{2,1,0:T(8,128)(2,1)S(1)} %collective-permute-done.1.refs_4_), channel_id=1, source_target_pairs={{0,12},{4,0},{8,4},{12,8},{1,13},{5,1},{9,5},{13,9},{2,14},{6,2},{... | collective-permute-start | bytes 786440 | tf_op jit(solution)/shard_map/ppermute | solution.py:223
  80.8 2.5 %collective-permute-done.2.refs_1_ = bf16[1,128,1024]{2,1,0:T(8,128)(2,1)S(1)} collective-permute-done((bf16[1,128,1024]{2,1,0:T(8,128)(2,1)S(1)}, bf16[1,128,1024]{2,1,0:T(8,128)(2,1)S(1)}, u32[]{:S(2)}, u32[]{:S(2)}) %collective-permute-start.2) | collective-permute-done | bytes 262176 | tf_op jit(solution)/shard_map/ppermute | solution.py:223
  83.3 2.9 %collective-permute-start.7 = (bf16[1,128,1024]{2,1,0:T(8,128)(2,1)S(1)}, bf16[1,128,1024]{2,1,0:T(8,128)(2,1)S(1)}, u32[]{:S(2)}, u32[]{:S(2)}) collective-permute-start(bf16[1,128,1024]{2,1,0:T(8,128)(2,1)S(1)} %collective-permute-done.1.refs_4_), channel_id=1, source_target_pairs={{0,8},{4,12},{8,0},{12,4},{1,9},{5,13},{9,1},{13,5},{2,10},{6,14},... | collective-permute-start | bytes 786440 | tf_op jit(solution)/shard_map/ppermute | solution.py:223
  86.3 4.4 %collective-permute-done.3.refs_2_ = bf16[1,128,1024]{2,1,0:T(8,128)(2,1)S(1)} collective-permute-done((bf16[1,128,1024]{2,1,0:T(8,128)(2,1)S(1)}, bf16[1,128,1024]{2,1,0:T(8,128)(2,1)S(1)}, u32[]{:S(2)}, u32[]{:S(2)}) %collective-permute-start.3) | collective-permute-done | bytes 262176 | tf_op jit(solution)/shard_map/ppermute | solution.py:223
  90.8 2.5 %collective-permute-done.7.refs_7_ = bf16[1,128,1024]{2,1,0:T(8,128)(2,1)S(1)} collective-permute-done((bf16[1,128,1024]{2,1,0:T(8,128)(2,1)S(1)}, bf16[1,128,1024]{2,1,0:T(8,128)(2,1)S(1)}, u32[]{:S(2)}, u32[]{:S(2)}) %collective-permute-start.7) | collective-permute-done | bytes 262176 | tf_op jit(solution)/shard_map/ppermute | solution.py:223
  99.4 4.7 %fusion.22 = f32[128,4096]{1,0:T(8,128)S(1)} fusion(bf16[1024,4096]{1,0:T(8,128)(2,1)} %param.21, bf16[1,128,1024]{2,1,0:T(8,128)(2,1)} %copy-done), kind=kOutput, calls=%fused_computation.36 | convolution fusion | flops 1073741824 | bytes 10747904 | tf_op jit(solution)/shard_map/dot_general | solution.py:375
  104.2 12.5 %collective-permute-done.12.refs_0_.refs_6_ = bf16[4,128,1024]{2,1,0:T(8,128)(2,1)S(1)} collective-permute-done((bf16[4,128,1024]{2,1,0:T(8,128)(2,1)}, bf16[4,128,1024]{2,1,0:T(8,128)(2,1)S(1)}, u32[]{:S(2)}, u32[]{:S(2)}) %collective-permute-start.12) | collective-permute-done | bytes 1048608 | tf_op jit(solution)/shard_map/ppermute | solution.py:223
  116.7 3.1 %collective-permute-done.13.refs_1_.refs_7_ = bf16[4,128,1024]{2,1,0:T(8,128)(2,1)S(1)} collective-permute-done((bf16[4,128,1024]{2,1,0:T(8,128)(2,1)}, bf16[4,128,1024]{2,1,0:T(8,128)(2,1)S(1)}, u32[]{:S(2)}, u32[]{:S(2)}) %collective-permute-start.13) | collective-permute-done | bytes 1048608 | tf_op jit(solution)/shard_map/ppermute | solution.py:223
  126.6 6.0 %convolution_add_fusion = f32[128,4096]{1,0:T(8,128)} fusion(f32[128,4096]{1,0:T(8,128)S(1)} %fusion.22, bf16[1024,4096]{1,0:T(8,128)(2,1)} %collective-permute-done, bf16[1,128,1024]{2,1,0:T(8,128)(2,1)S(1)} %collective-permute-done.1.refs_4_), kind=kOutput, calls=%fused_computation.1 | convolution fusion | flops 1074266112 | bytes 12845056 | tf_op jit(solution)/shard_map/dot_general | solution.py:375
  134.6 3.1 %collective-permute-done.11.refs_4_ = bf16[2,128,1024]{2,1,0:T(8,128)(2,1)} collective-permute-done((bf16[2,128,1024]{2,1,0:T(8,128)(2,1)}, bf16[2,128,1024]{2,1,0:T(8,128)(2,1)}, u32[]{:S(2)}, u32[]{:S(2)}) %collective-permute-start.11) | collective-permute-done | bytes 524320 | tf_op jit(solution)/shard_map/ppermute | solution.py:223
  137.7 5.2 %hessian_tiles.5 = f32[3,512,512]{2,1,0:T(8,128)} custom-call(s32[36]{0:T(128)S(1)} %reshape.695.where_ref, bf16[4,128,1024]{2,1,0:T(8,128)(2,1)} %get-tuple-element.55.refs_0_, bf16[4,128,1024]{2,1,0:T(8,128)(2,1)S(1)} %collective-permute-done.8.refs_0_.refs_1_, bf16[4,128,1024]{2,1,0:T(8,128)(2,1)} %collective-permute-done.9.refs_1_.refs_2_, ...), custom_call_target="tpu_custom_call" | custom-call | flops 402653184 | bytes 6291456 | tf_op jit(solution)/shard_map/hessian_tiles/pallas_call | solution.py:275
  142.9 5.1 %collective-permute-start.16 = (f32[3,512,512]{2,1,0:T(8,128)}, f32[3,512,512]{2,1,0:T(8,128)}, u32[]{:S(2)}, u32[]{:S(2)}) collective-permute-start(f32[3,512,512]{2,1,0:T(8,128)} %hessian_tiles.5), channel_id=1, source_target_pairs={{0,1},{1,0},{2,3},{3,2},{4,5},{5,4},{6,7},{7,6},{8,9},{9,8},{10,11... | collective-permute-start | bytes 9437192 | tf_op jit(solution)/shard_map/ppermute | solution.py:223
  148.3 5.2 %hessian_tiles.6 = f32[3,512,512]{2,1,0:T(8,128)} custom-call(s32[36]{0:T(128)S(1)} %reshape.696.where_ref, bf16[4,128,1024]{2,1,0:T(8,128)(2,1)} %get-tuple-element.55.refs_0_, bf16[4,128,1024]{2,1,0:T(8,128)(2,1)S(1)} %collective-permute-done.8.refs_0_.refs_1_, bf16[4,128,1024]{2,1,0:T(8,128)(2,1)} %collective-permute-done.9.refs_1_.refs_2_, ...), custom_call_target="tpu_custom_call" | custom-call | flops 402653184 | bytes 6291456 | tf_op jit(solution)/shard_map/hessian_tiles/pallas_call | solution.py:275
  158.9 3.7 %fusion.15 = (f16[512,512]{1,0:T(8,128)(2,1)}, f16[512,512]{1,0:T(8,128)(2,1)}) fusion(f32[3,512,512]{2,1,0:T(8,128)} %collective-permute-done.16, f32[3,512,512]{2,1,0:T(8,128)} %hessian_tiles.6), kind=kLoop, calls=%fused_computation.25 | loop fusion | flops 1048576 | bytes 5242880 | tf_op jit(solution)/shard_map/convert_element_type | solution.py:397
  162.7 7.2 %hessian_tiles.7 = f32[5,512,512]{2,1,0:T(8,128)} custom-call(s32[60]{0:T(128)S(1)} %reshape.697.where_ref, bf16[4,128,1024]{2,1,0:T(8,128)(2,1)} %get-tuple-element.55.refs_0_, bf16[4,128,1024]{2,1,0:T(8,128)(2,1)S(1)} %collective-permute-done.8.refs_0_.refs_1_, bf16[4,128,1024]{2,1,0:T(8,128)(2,1)} %collective-permute-done.9.refs_1_.refs_2_, ...), custom_call_target="tpu_custom_call" | custom-call | flops 671088640 | bytes 10485760 | tf_op jit(solution)/shard_map/hessian_tiles/pallas_call | solution.py:275
  170.0 2.7 %fusion.19 = (f16[512,512]{1,0:T(8,128)(2,1)}, f16[512,512]{1,0:T(8,128)(2,1)}) fusion(f16[512,512]{1,0:T(8,128)(2,1)} %get-tuple-element.74, f32[3,512,512]{2,1,0:T(8,128)} %collective-permute-done.16, f32[3,512,512]{2,1,0:T(8,128)} %hessian_tiles.6, f16[256,512]{1,0:T(8,128)(2,1)S(1)} %collective-permute-done.17, f16[512,512]{1,0:T(8,128)(2,1)} %get-tuple-element.76, ...), kind=kLoop, calls=%fused_computation.33 | loop fusion | flops 1048576 | bytes 3145728 | tf_op jit(solution)/shard_map/dynamic_update_slice | solution.py:412
  172.7 2.7 %collective-permute-start.23 = (f16[512,512]{1,0:T(8,128)(2,1)}, f16[512,512]{1,0:T(8,128)(2,1)}, u32[]{:S(2)}, u32[]{:S(2)}) collective-permute-start(f16[512,512]{1,0:T(8,128)(2,1)} %get-tuple-element.87), channel_id=1, source_target_pairs={{0,112},{16,0},{32,16},{48,32},{64,48},{80,64},{96,80},{112,96},{1... | collective-permute-start | bytes 1572872 | tf_op jit(solution)/shard_map/ppermute | solution.py:223
  175.7 5.1 %hessian_tiles.4 = f32[5,512,512]{2,1,0:T(8,128)S(1)} custom-call(s32[60]{0:T(128)S(1)} %reshape.694.where_ref, bf16[4,128,1024]{2,1,0:T(8,128)(2,1)} %get-tuple-element.55.refs_0_, bf16[4,128,1024]{2,1,0:T(8,128)(2,1)S(1)} %collective-permute-done.8.refs_0_.refs_1_, bf16[4,128,1024]{2,1,0:T(8,128)(2,1)} %collective-permute-done.9.refs_1_.refs_2_, ...), custom_call_target="tpu_custom_call" | custom-call | flops 671088640 | bytes 10485760 | tf_op jit(solution)/shard_map/hessian_tiles/pallas_call | solution.py:275
  180.8 6.4 %collective-permute-done.20 = f16[512,512]{1,0:T(8,128)(2,1)} collective-permute-done((f16[512,512]{1,0:T(8,128)(2,1)}, f16[512,512]{1,0:T(8,128)(2,1)}, u32[]{:S(2)}, u32[]{:S(2)}) %collective-permute-start.20) | collective-permute-done | bytes 524320 | tf_op jit(solution)/shard_map/ppermute | solution.py:223
  190.7 2.7 %collective-permute-start.24 = (f16[512,512]{1,0:T(8,128)(2,1)S(1)}, f16[512,512]{1,0:T(8,128)(2,1)S(1)}, u32[]{:S(2)}, u32[]{:S(2)}) collective-permute-start(f16[512,512]{1,0:T(8,128)(2,1)S(1)} %fusion.13), channel_id=1, source_target_pairs={{0,112},{16,0},{32,16},{48,32},{64,48},{80,64},{96,80},{112,96},{1... | collective-permute-start | bytes 1572872 | tf_op jit(solution)/shard_map/ppermute | solution.py:223
  193.4 9.0 %collective-permute-done.21 = f16[512,512]{1,0:T(8,128)(2,1)S(1)} collective-permute-done((f16[512,512]{1,0:T(8,128)(2,1)S(1)}, f16[512,512]{1,0:T(8,128)(2,1)S(1)}, u32[]{:S(2)}, u32[]{:S(2)}) %collective-permute-start.21) | collective-permute-done | bytes 524320 | tf_op jit(solution)/shard_map/ppermute | solution.py:223
  205.6 2.7 %collective-permute-start.25 = (f16[512,512]{1,0:T(8,128)(2,1)S(1)}, f16[512,512]{1,0:T(8,128)(2,1)S(1)}, u32[]{:S(2)}, u32[]{:S(2)}) collective-permute-start(f16[512,512]{1,0:T(8,128)(2,1)S(1)} %fusion.12), channel_id=1, source_target_pairs={{0,112},{16,0},{32,16},{48,32},{64,48},{80,64},{96,80},{112,96},{1... | collective-permute-start | bytes 1572872 | tf_op jit(solution)/shard_map/ppermute | solution.py:223
  208.3 8.3 %collective-permute-done.22 = f16[512,512]{1,0:T(8,128)(2,1)S(1)} collective-permute-done((f16[512,512]{1,0:T(8,128)(2,1)S(1)}, f16[512,512]{1,0:T(8,128)(2,1)S(1)}, u32[]{:S(2)}, u32[]{:S(2)}) %collective-permute-start.22) | collective-permute-done | bytes 524320 | tf_op jit(solution)/shard_map/ppermute | solution.py:223
  217.1 2.6 %fusion.10 = f32[1,512,512]{2,1,0:T(8,128)} fusion(f32[5,512,512]{2,1,0:T(8,128)} %collective-permute-done.19, f32[5,512,512]{2,1,0:T(8,128)S(1)} %hessian_tiles.4, f16[512,512]{1,0:T(8,128)(2,1)S(1)} %collective-permute-done.25, f16[512,512]{1,0:T(8,128)(2,1)S(1)} %collective-permute-done.22), kind=kLoop, calls=%fused_computation.15 | loop fusion | flops 1572864 | bytes 4194304 | tf_op jit(solution)/shard_map/broadcast_in_dim | solution.py:420
  (115 shorter events, 43.2 us)
Async XLA Ops:
  7.2 38.2 %copy-start.2 = (f32[16,64,256]{2,1,0:T(8,128)S(1)}, f32[16,64,256]{2,1,0:T(8,128)}, u32[]{:S(2)}) copy-start(f32[16,64,256]{2,1,0:T(8,128)} %param.19) | copy-start | bytes 3145732
  7.2 38.1 %collective-permute-start = (bf16[1024,4096]{1,0:T(8,128)(2,1)}, bf16[1024,4096]{1,0:T(8,128)(2,1)}, u32[]{:S(2)}, u32[]{:S(2)}) collective-permute-start(bf16[1024,4096]{1,0:T(8,128)(2,1)} %param.21), channel_id=1, source_target_pairs={{0,1},{1,0},{2,3},{3,2},{4,5},{5,4},{6,7},{7,6},{8,9},{9,8},{10,11... | collective-permute-start | bytes 25165832 | tf_op jit(solution)/shard_map/ppermute | solution.py:223
  17.2 36.6 %copy-start.1 = (bf16[256,2048]{1,0:T(8,128)(2,1)S(1)}, bf16[256,2048]{1,0:T(8,128)(2,1)}, u32[]{:S(2)}) copy-start(bf16[256,2048]{1,0:T(8,128)(2,1)} %c_ref.3) | copy-start | bytes 3145732
  17.2 36.6 %copy-start.4 = (bf16[256,2048]{1,0:T(8,128)(2,1)S(1)}, bf16[256,2048]{1,0:T(8,128)(2,1)}, u32[]{:S(2)}) copy-start(bf16[256,2048]{1,0:T(8,128)(2,1)} %b_ref.3) | copy-start | bytes 3145732
  17.2 36.6 %copy-start.9 = (f32[256,16]{0,1:T(8,128)S(1)}, f32[256,16]{0,1:T(8,128)}, u32[]{:S(2)}) copy-start(f32[256,16]{0,1:T(8,128)} %param.16) | copy-start | bytes 49156
  48.3 19.1 %all-to-all-start.1 = ((f16[16,136,128]{2,1,0:T(8,128)(2,1)}), f16[16,136,128]{2,1,0:T(8,128)(2,1)}, u32[]{:S(2)}, u32[]{:S(2)}) async-start(f16[16,136,128]{2,1,0:T(8,128)(2,1)} %convert_element_type.112), calls=%async_computation.1 | async-start | bytes 1114112 | tf_op jit(solution)/shard_map/all_to_all | solution.py:334
  52.6 167.6 %reduce-scatter.2.cloned.1.call-start = ((), (), s32[]{:S(2)}) async-start(), calls=%async_computation.3 | async-start | bytes 2359296 | tf_op jit(solution)/shard_map/reduce_scatter | solution.py:379
  72.0 6.1 %collective-permute-start.1 = (bf16[1,128,1024]{2,1,0:T(8,128)(2,1)S(1)}, bf16[1,128,1024]{2,1,0:T(8,128)(2,1)S(1)}, u32[]{:S(2)}, u32[]{:S(2)}) collective-permute-start(bf16[1,128,1024]{2,1,0:T(8,128)(2,1)S(1)} %get-tuple-element.46), channel_id=1, source_target_pairs={{0,1},{1,0},{2,3},{3,2},{4,5},{5,4},{6,7},{7,6},{8,9},{9,8},{10,11... | collective-permute-start | bytes 786440 | tf_op jit(solution)/shard_map/ppermute | solution.py:223
  75.5 7.9 %collective-permute-start.2 = (bf16[1,128,1024]{2,1,0:T(8,128)(2,1)S(1)}, bf16[1,128,1024]{2,1,0:T(8,128)(2,1)S(1)}, u32[]{:S(2)}, u32[]{:S(2)}) collective-permute-start(bf16[1,128,1024]{2,1,0:T(8,128)(2,1)S(1)} %get-tuple-element.45.refs_0_), channel_id=1, source_target_pairs={{0,130},{2,0},{128,2},{130,128},{1,131},{3,1},{129,3},{131,129},{4... | collective-permute-start | bytes 786440 | tf_op jit(solution)/shard_map/ppermute | solution.py:223
  76.3 14.4 %collective-permute-start.3 = (bf16[1,128,1024]{2,1,0:T(8,128)(2,1)S(1)}, bf16[1,128,1024]{2,1,0:T(8,128)(2,1)S(1)}, u32[]{:S(2)}, u32[]{:S(2)}) collective-permute-start(bf16[1,128,1024]{2,1,0:T(8,128)(2,1)S(1)} %get-tuple-element.45.refs_0_), channel_id=1, source_target_pairs={{0,2},{2,128},{128,130},{130,0},{1,3},{3,129},{129,131},{131,1},{4... | collective-permute-start | bytes 786440 | tf_op jit(solution)/shard_map/ppermute | solution.py:223
  77.1 13.7 %collective-permute-start.4 = (bf16[1,128,1024]{2,1,0:T(8,128)(2,1)S(1)}, bf16[1,128,1024]{2,1,0:T(8,128)(2,1)S(1)}, u32[]{:S(2)}, u32[]{:S(2)}) collective-permute-start(bf16[1,128,1024]{2,1,0:T(8,128)(2,1)S(1)} %get-tuple-element.45.refs_0_), channel_id=1, source_target_pairs={{0,128},{2,130},{128,0},{130,2},{1,129},{3,131},{129,1},{131,3},{4... | collective-permute-start | bytes 786440 | tf_op jit(solution)/shard_map/ppermute | solution.py:223
  78.1 12.7 %collective-permute-start.5 = (bf16[1,128,1024]{2,1,0:T(8,128)(2,1)S(1)}, bf16[1,128,1024]{2,1,0:T(8,128)(2,1)S(1)}, u32[]{:S(2)}, u32[]{:S(2)}) collective-permute-start(bf16[1,128,1024]{2,1,0:T(8,128)(2,1)S(1)} %collective-permute-done.1.refs_4_), channel_id=1, source_target_pairs={{0,12},{4,0},{8,4},{12,8},{1,13},{5,1},{9,5},{13,9},{2,14},{6,2},{... | collective-permute-start | bytes 786440 | tf_op jit(solution)/shard_map/ppermute | solution.py:223
  80.8 9.9 %collective-permute-start.6 = (bf16[1,128,1024]{2,1,0:T(8,128)(2,1)S(1)}, bf16[1,128,1024]{2,1,0:T(8,128)(2,1)S(1)}, u32[]{:S(2)}, u32[]{:S(2)}) collective-permute-start(bf16[1,128,1024]{2,1,0:T(8,128)(2,1)S(1)} %collective-permute-done.1.refs_4_), channel_id=1, source_target_pairs={{0,4},{4,8},{8,12},{12,0},{1,5},{5,9},{9,13},{13,1},{2,6},{6,10},{... | collective-permute-start | bytes 786440 | tf_op jit(solution)/shard_map/ppermute | solution.py:223
  83.3 9.9 %collective-permute-start.7 = (bf16[1,128,1024]{2,1,0:T(8,128)(2,1)S(1)}, bf16[1,128,1024]{2,1,0:T(8,128)(2,1)S(1)}, u32[]{:S(2)}, u32[]{:S(2)}) collective-permute-start(bf16[1,128,1024]{2,1,0:T(8,128)(2,1)S(1)} %collective-permute-done.1.refs_4_), channel_id=1, source_target_pairs={{0,8},{4,12},{8,0},{12,4},{1,9},{5,13},{9,1},{13,5},{2,10},{6,14},... | collective-permute-start | bytes 786440 | tf_op jit(solution)/shard_map/ppermute | solution.py:223
  94.8 22.0 %collective-permute-start.12 = (bf16[4,128,1024]{2,1,0:T(8,128)(2,1)}, bf16[4,128,1024]{2,1,0:T(8,128)(2,1)S(1)}, u32[]{:S(2)}, u32[]{:S(2)}) collective-permute-start(bf16[4,128,1024]{2,1,0:T(8,128)(2,1)} %get-tuple-element.60.refs_5_), channel_id=1, source_target_pairs={{0,130},{2,0},{128,2},{130,128},{1,131},{3,1},{129,3},{131,129},{4... | collective-permute-start | bytes 3145736 | tf_op jit(solution)/shard_map/ppermute | solution.py:223
  96.7 23.1 %collective-permute-start.13 = (bf16[4,128,1024]{2,1,0:T(8,128)(2,1)}, bf16[4,128,1024]{2,1,0:T(8,128)(2,1)S(1)}, u32[]{:S(2)}, u32[]{:S(2)}) collective-permute-start(bf16[4,128,1024]{2,1,0:T(8,128)(2,1)} %get-tuple-element.60.refs_5_), channel_id=1, source_target_pairs={{0,2},{2,128},{128,130},{130,0},{1,3},{3,129},{129,131},{131,1},{4... | collective-permute-start | bytes 3145736 | tf_op jit(solution)/shard_map/ppermute | solution.py:223
  96.7 25.6 %collective-permute-start.8 = (bf16[4,128,1024]{2,1,0:T(8,128)(2,1)}, bf16[4,128,1024]{2,1,0:T(8,128)(2,1)S(1)}, u32[]{:S(2)}, u32[]{:S(2)}) collective-permute-start(bf16[4,128,1024]{2,1,0:T(8,128)(2,1)} %get-tuple-element.55.refs_0_), channel_id=1, source_target_pairs={{0,12},{4,0},{8,4},{12,8},{1,13},{5,1},{9,5},{13,9},{2,14},{6,2},{... | collective-permute-start | bytes 3145736 | tf_op jit(solution)/shard_map/ppermute | solution.py:223
  97.9 24.4 %collective-permute-start.9 = (bf16[4,128,1024]{2,1,0:T(8,128)(2,1)}, bf16[4,128,1024]{2,1,0:T(8,128)(2,1)}, u32[]{:S(2)}, u32[]{:S(2)}) collective-permute-start(bf16[4,128,1024]{2,1,0:T(8,128)(2,1)} %get-tuple-element.55.refs_0_), channel_id=1, source_target_pairs={{0,4},{4,8},{8,12},{12,0},{1,5},{5,9},{9,13},{13,1},{2,6},{6,10},{... | collective-permute-start | bytes 3145736 | tf_op jit(solution)/shard_map/ppermute | solution.py:223
  120.9 11.8 %collective-permute-start.14 = (bf16[2,128,1024]{2,1,0:T(8,128)(2,1)}, bf16[2,128,1024]{2,1,0:T(8,128)(2,1)}, u32[]{:S(2)}, u32[]{:S(2)}) collective-permute-start(bf16[2,128,1024]{2,1,0:T(8,128)(2,1)} %get-tuple-element.52), channel_id=1, source_target_pairs={{0,130},{2,0},{128,2},{130,128},{1,131},{3,1},{129,3},{131,129},{4... | collective-permute-start | bytes 1572872 | tf_op jit(solution)/shard_map/ppermute | solution.py:223
  121.2 11.5 %collective-permute-start.15 = (bf16[2,128,1024]{2,1,0:T(8,128)(2,1)}, bf16[2,128,1024]{2,1,0:T(8,128)(2,1)}, u32[]{:S(2)}, u32[]{:S(2)}) collective-permute-start(bf16[2,128,1024]{2,1,0:T(8,128)(2,1)} %get-tuple-element.53), channel_id=1, source_target_pairs={{0,2},{2,128},{128,130},{130,0},{1,3},{3,129},{129,131},{131,1},{4... | collective-permute-start | bytes 1572872 | tf_op jit(solution)/shard_map/ppermute | solution.py:223
  124.6 10.0 %collective-permute-start.10 = (bf16[2,128,1024]{2,1,0:T(8,128)(2,1)}, bf16[2,128,1024]{2,1,0:T(8,128)(2,1)}, u32[]{:S(2)}, u32[]{:S(2)}) collective-permute-start(bf16[2,128,1024]{2,1,0:T(8,128)(2,1)} %get-tuple-element.49), channel_id=1, source_target_pairs={{0,12},{4,0},{8,4},{12,8},{1,13},{5,1},{9,5},{13,9},{2,14},{6,2},{... | collective-permute-start | bytes 1572872 | tf_op jit(solution)/shard_map/ppermute | solution.py:223
  126.6 11.1 %collective-permute-start.11 = (bf16[2,128,1024]{2,1,0:T(8,128)(2,1)}, bf16[2,128,1024]{2,1,0:T(8,128)(2,1)}, u32[]{:S(2)}, u32[]{:S(2)}) collective-permute-start(bf16[2,128,1024]{2,1,0:T(8,128)(2,1)} %get-tuple-element.50), channel_id=1, source_target_pairs={{0,4},{4,8},{8,12},{12,0},{1,5},{5,9},{9,13},{13,1},{2,6},{6,10},{... | collective-permute-start | bytes 1572872 | tf_op jit(solution)/shard_map/ppermute | solution.py:223
  142.9 10.7 %collective-permute-start.16 = (f32[3,512,512]{2,1,0:T(8,128)}, f32[3,512,512]{2,1,0:T(8,128)}, u32[]{:S(2)}, u32[]{:S(2)}) collective-permute-start(f32[3,512,512]{2,1,0:T(8,128)} %hessian_tiles.5), channel_id=1, source_target_pairs={{0,1},{1,0},{2,3},{3,2},{4,5},{5,4},{6,7},{7,6},{8,9},{9,8},{10,11... | collective-permute-start | bytes 9437192 | tf_op jit(solution)/shard_map/ppermute | solution.py:223
  156.3 13.6 %collective-permute-start.17 = (f16[256,512]{1,0:T(8,128)(2,1)}, f16[256,512]{1,0:T(8,128)(2,1)S(1)}, u32[]{:S(2)}, u32[]{:S(2)}) collective-permute-start(f16[256,512]{1,0:T(8,128)(2,1)} %get-tuple-element.91), channel_id=1, source_target_pairs={{0,16},{16,32},{32,48},{48,64},{64,80},{80,96},{96,112},{112,0},{1... | collective-permute-start | bytes 786440 | tf_op jit(solution)/shard_map/ppermute | solution.py:223
  157.2 12.7 %collective-permute-start.18 = (f16[256,512]{1,0:T(8,128)(2,1)}, f16[256,512]{1,0:T(8,128)(2,1)}, u32[]{:S(2)}, u32[]{:S(2)}) collective-permute-start(f16[256,512]{1,0:T(8,128)(2,1)} %get-tuple-element.90), channel_id=1, source_target_pairs={{0,112},{16,0},{32,16},{48,32},{64,48},{80,64},{96,80},{112,96},{1... | collective-permute-start | bytes 786440 | tf_op jit(solution)/shard_map/ppermute | solution.py:223
  169.9 17.3 %collective-permute-start.19 = (f32[5,512,512]{2,1,0:T(8,128)}, f32[5,512,512]{2,1,0:T(8,128)}, u32[]{:S(2)}, u32[]{:S(2)}) collective-permute-start(f32[5,512,512]{2,1,0:T(8,128)} %hessian_tiles.7), channel_id=1, source_target_pairs={{0,1},{1,0},{2,3},{3,2},{4,5},{5,4},{6,7},{7,6},{8,9},{9,8},{10,11... | collective-permute-start | bytes 15728648 | tf_op jit(solution)/shard_map/ppermute | solution.py:223
  172.7 14.5 %collective-permute-start.20 = (f16[512,512]{1,0:T(8,128)(2,1)}, f16[512,512]{1,0:T(8,128)(2,1)}, u32[]{:S(2)}, u32[]{:S(2)}) collective-permute-start(f16[512,512]{1,0:T(8,128)(2,1)} %get-tuple-element.86), channel_id=1, source_target_pairs={{0,16},{16,32},{32,48},{48,64},{64,80},{80,96},{96,112},{112,0},{1... | collective-permute-start | bytes 1572872 | tf_op jit(solution)/shard_map/ppermute | solution.py:223
  172.7 16.3 %collective-permute-start.23 = (f16[512,512]{1,0:T(8,128)(2,1)}, f16[512,512]{1,0:T(8,128)(2,1)}, u32[]{:S(2)}, u32[]{:S(2)}) collective-permute-start(f16[512,512]{1,0:T(8,128)(2,1)} %get-tuple-element.87), channel_id=1, source_target_pairs={{0,112},{16,0},{32,16},{48,32},{64,48},{80,64},{96,80},{112,96},{1... | collective-permute-start | bytes 1572872 | tf_op jit(solution)/shard_map/ppermute | solution.py:223
  188.9 13.5 %collective-permute-start.21 = (f16[512,512]{1,0:T(8,128)(2,1)S(1)}, f16[512,512]{1,0:T(8,128)(2,1)S(1)}, u32[]{:S(2)}, u32[]{:S(2)}) collective-permute-start(f16[512,512]{1,0:T(8,128)(2,1)S(1)} %fusion.5), channel_id=1, source_target_pairs={{0,16},{16,32},{32,48},{48,64},{64,80},{80,96},{96,112},{112,0},{1... | collective-permute-start | bytes 1572872 | tf_op jit(solution)/shard_map/ppermute | solution.py:223
  190.7 13.4 %collective-permute-start.24 = (f16[512,512]{1,0:T(8,128)(2,1)S(1)}, f16[512,512]{1,0:T(8,128)(2,1)S(1)}, u32[]{:S(2)}, u32[]{:S(2)}) collective-permute-start(f16[512,512]{1,0:T(8,128)(2,1)S(1)} %fusion.13), channel_id=1, source_target_pairs={{0,112},{16,0},{32,16},{48,32},{64,48},{80,64},{96,80},{112,96},{1... | collective-permute-start | bytes 1572872 | tf_op jit(solution)/shard_map/ppermute | solution.py:223
  204.0 12.7 %collective-permute-start.22 = (f16[512,512]{1,0:T(8,128)(2,1)S(1)}, f16[512,512]{1,0:T(8,128)(2,1)S(1)}, u32[]{:S(2)}, u32[]{:S(2)}) collective-permute-start(f16[512,512]{1,0:T(8,128)(2,1)S(1)} %fusion.2), channel_id=1, source_target_pairs={{0,16},{16,32},{32,48},{48,64},{64,80},{80,96},{96,112},{112,0},{1... | collective-permute-start | bytes 1572872 | tf_op jit(solution)/shard_map/ppermute | solution.py:223
  205.6 11.5 %collective-permute-start.25 = (f16[512,512]{1,0:T(8,128)(2,1)S(1)}, f16[512,512]{1,0:T(8,128)(2,1)S(1)}, u32[]{:S(2)}, u32[]{:S(2)}) collective-permute-start(f16[512,512]{1,0:T(8,128)(2,1)S(1)} %fusion.12), channel_id=1, source_target_pairs={{0,112},{16,0},{32,16},{48,32},{64,48},{80,64},{96,80},{112,96},{1... | collective-permute-start | bytes 1572872 | tf_op jit(solution)/shard_map/ppermute | solution.py:223
  (11 other events, 159.7 us)
Sparse Core Ops, SparseCore 0:
  170.2 49.9 reduce-scatter.1

commit v2 on v1

--- a/solution.py
+++ b/solution.py
@@ -25,7 +25,7 @@
 LAST = 1000.0
 PAY = HEADS // 2 * 16 + 8
 ORDER = (4, 3, 5, 2, 6, 1, 7, 0)
-VMEM = 24 * 1024 * 1024
+VMEM = 16 * 1024 * 1024
 SOURCES = 10
 TILE_SCALE = 2.0**-8
 

time: 230 us -> 231 us (level)
  transfers between devices with their start and end apart: 28 -> 28, of which waited for: 14 -> 13; matrix products, arithmetic and copies ran while one was open for 13% -> 13% of each run, Pallas kernels for 11% -> 11%
where the time goes in v2:
time: 231 us; the launch traced here: 229 us
  waiting for transfers between devices  66.2 us (29%)
  starting transfers between devices  43.8 us (19%)
  Pallas kernels  35.6 us (15%)
  blocking collectives  28 us (12%)
  other arithmetic  20.9 us (9%)
  between operations  14.5 us (6%)
  matrix products  10.9 us (5%)
  local copies, waits for them, and re-layouts  8.81 us (4%)
    ppermute x26, waiting for transfers between devices, moved(): return lax.ppermute(v, axis, [(i, (i - by) % n) for i in range(n)])  56.5 us
    ppermute x26, starting transfers between devices, moved(): return lax.ppermute(v, axis, [(i, (i - by) % n) for i in range(n)])  39.5 us
    all_to_all x1, blocking collectives, body(): sent = lax.all_to_all(sent.astype(F16), CTX, 0, 0, tiled=True)  28 us
    pallas_call x4, Pallas kernels, make_tiles(): pl.pallas_call(functools.partial(tile_kernel, counts), grid_spec=pltpu.Pr...  21.3 us
    all_to_all x1, waiting for transfers between devices, body(): lax.all_to_all(incoming.astype(F16), CTX, 0, 0, tiled=True).astype(F32)  9.65 us
    dot_general x1, matrix products, body(): jnp.dot(got[0], w_other, preferred_element_type=F32)  6.12 us
    unnamed x30, local copies, waits for them, and re-layouts  5.77 us
    dot_general x1, matrix products, body(): jnp.dot(keep[0], w_out, preferred_element_type=F32)  4.74 us
  transfers between devices with their start and end apart: 28, of which 13 were waited for; matrix products, arithmetic and copies ran while one was open for 13% of the time, Pallas kernels for 11%

profile of v2, /device:TPU:1, one launch (start us, length us, event | category | flops | bytes accessed | tf_op | source)
XLA Modules:
  0.0 228.6 jit_solution(8207752430360088247)
XLA Ops:
  7.2 3.3 %collective-permute-start = (bf16[1024,4096]{1,0:T(8,128)(2,1)}, bf16[1024,4096]{1,0:T(8,128)(2,1)}, u32[]{:S(2)}, u32[]{:S(2)}) collective-permute-start(bf16[1024,4096]{1,0:T(8,128)(2,1)} %param.21), channel_id=1, source_target_pairs={{0,1},{1,0},{2,3},{3,2},{4,5},{5,4},{6,7},{7,6},{8,9},{9,8},{10,11... | collective-permute-start | bytes 25165832 | tf_op jit(solution)/shard_map/ppermute | solution.py:223
  14.2 2.9 %mixer_start.1 = (f32[16,136,128]{2,1,0:T(8,128)S(1)}, f32[256,16]{1,0:T(8,128)S(1)}, f32[16,256]{1,0:T(8,128)S(1)}) custom-call(s32[3]{0:T(128)S(1)} %pad_add_fusion.2.g_ref.at_ref, bf16[256,1024]{1,0:T(8,128)(2,1)S(1)} %copy-done.6, bf16[256,2048]{1,0:T(8,128)(2,1)S(1)} %copy-done.3, f32[16,256]{1,0:T(8,128)S(1)} %bitcast.126, f32[1,16]{1,0:T(1,128)S(1)} %bitcast.129), custom_call_target="tpu_custom_call" | custom-call | tf_op jit(solution)/shard_map/mixer_start/pallas_call | solution.py:304
  17.3 28.0 %all_to_all.10 = f16[16,136,128]{2,1,0:T(8,128)(2,1)S(1)} all-to-all(f16[16,136,128]{2,1,0:T(8,128)(2,1)S(1)} %convert_element_type.110), channel_id=1, replica_groups=mesh['x_hi'=2,'z'=8,'y'=4,'x_lo'=2,'core'=2] {'x_hi','z'}, dimensions={0} | all-to-all | bytes 1114112 | tf_op jit(solution)/shard_map/all_to_all | solution.py:319
  48.3 4.3 %all-to-all-start.1 = ((f16[16,136,128]{2,1,0:T(8,128)(2,1)}), f16[16,136,128]{2,1,0:T(8,128)(2,1)}, u32[]{:S(2)}, u32[]{:S(2)}) async-start(f16[16,136,128]{2,1,0:T(8,128)(2,1)} %convert_element_type.112), calls=%async_computation.1 | async-start | bytes 1114112 | tf_op jit(solution)/shard_map/all_to_all | solution.py:334
  54.9 2.3 mixer_inner.1.y_ref
  57.7 9.7 %all-to-all-done.1 = f16[16,136,128]{2,1,0:T(8,128)(2,1)} async-done(((f16[16,136,128]{2,1,0:T(8,128)(2,1)}), f16[16,136,128]{2,1,0:T(8,128)(2,1)}, u32[]{:S(2)}, u32[]{:S(2)}) %all-to-all-start.1) | async-done | bytes 557088 | tf_op jit(solution)/shard_map/all_to_all | solution.py:334
  69.6 2.4 %mixer_finish.1 = (bf16[1,128,1024]{2,1,0:T(8,128)(2,1)S(1)}, bf16[1,128,1024]{2,1,0:T(8,128)(2,1)S(1)}) custom-call(s32[3]{0:T(128)S(1)} %pad_add_fusion.2.g_ref.at_ref, f32[256,1024]{1,0:T(8,128)S(1)} %mixer_inner.1.y_ref, bf16[256,1024]{1,0:T(8,128)(2,1)S(1)} %copy-done.5, bf16[256,2048]{1,0:T(8,128)(2,1)S(1)} %copy-done.1, ...), custom_call_target="tpu_custom_call" | custom-call | tf_op jit(solution)/shard_map/mixer_finish/pallas_call | solution.py:354
  72.0 3.5 %collective-permute-start.1 = (bf16[1,128,1024]{2,1,0:T(8,128)(2,1)S(1)}, bf16[1,128,1024]{2,1,0:T(8,128)(2,1)S(1)}, u32[]{:S(2)}, u32[]{:S(2)}) collective-permute-start(bf16[1,128,1024]{2,1,0:T(8,128)(2,1)S(1)} %get-tuple-element.46), channel_id=1, source_target_pairs={{0,1},{1,0},{2,3},{3,2},{4,5},{5,4},{6,7},{7,6},{8,9},{9,8},{10,11... | collective-permute-start | bytes 786440 | tf_op jit(solution)/shard_map/ppermute | solution.py:223
  78.1 2.8 %collective-permute-start.5 = (bf16[1,128,1024]{2,1,0:T(8,128)(2,1)S(1)}, bf16[1,128,1024]{2,1,0:T(8,128)(2,1)S(1)}, u32[]{:S(2)}, u32[]{:S(2)}) collective-permute-start(bf16[1,128,1024]{2,1,0:T(8,128)(2,1)S(1)} %collective-permute-done.1.refs_4_), channel_id=1, source_target_pairs={{0,12},{4,0},{8,4},{12,8},{1,13},{5,1},{9,5},{13,9},{2,14},{6,2},{... | collective-permute-start | bytes 786440 | tf_op jit(solution)/shard_map/ppermute | solution.py:223
  80.8 2.5 %collective-permute-done.2.refs_1_ = bf16[1,128,1024]{2,1,0:T(8,128)(2,1)S(1)} collective-permute-done((bf16[1,128,1024]{2,1,0:T(8,128)(2,1)S(1)}, bf16[1,128,1024]{2,1,0:T(8,128)(2,1)S(1)}, u32[]{:S(2)}, u32[]{:S(2)}) %collective-permute-start.2) | collective-permute-done | bytes 262176 | tf_op jit(solution)/shard_map/ppermute | solution.py:223
  83.3 2.9 %collective-permute-start.7 = (bf16[1,128,1024]{2,1,0:T(8,128)(2,1)S(1)}, bf16[1,128,1024]{2,1,0:T(8,128)(2,1)S(1)}, u32[]{:S(2)}, u32[]{:S(2)}) collective-permute-start(bf16[1,128,1024]{2,1,0:T(8,128)(2,1)S(1)} %collective-permute-done.1.refs_4_), channel_id=1, source_target_pairs={{0,8},{4,12},{8,0},{12,4},{1,9},{5,13},{9,1},{13,5},{2,10},{6,14},... | collective-permute-start | bytes 786440 | tf_op jit(solution)/shard_map/ppermute | solution.py:223
  86.3 4.4 %collective-permute-done.3.refs_2_ = bf16[1,128,1024]{2,1,0:T(8,128)(2,1)S(1)} collective-permute-done((bf16[1,128,1024]{2,1,0:T(8,128)(2,1)S(1)}, bf16[1,128,1024]{2,1,0:T(8,128)(2,1)S(1)}, u32[]{:S(2)}, u32[]{:S(2)}) %collective-permute-start.3) | collective-permute-done | bytes 262176 | tf_op jit(solution)/shard_map/ppermute | solution.py:223
  90.8 2.5 %collective-permute-done.7.refs_7_ = bf16[1,128,1024]{2,1,0:T(8,128)(2,1)S(1)} collective-permute-done((bf16[1,128,1024]{2,1,0:T(8,128)(2,1)S(1)}, bf16[1,128,1024]{2,1,0:T(8,128)(2,1)S(1)}, u32[]{:S(2)}, u32[]{:S(2)}) %collective-permute-start.7) | collective-permute-done | bytes 262176 | tf_op jit(solution)/shard_map/ppermute | solution.py:223
  99.4 4.7 %fusion.22 = f32[128,4096]{1,0:T(8,128)S(1)} fusion(bf16[1024,4096]{1,0:T(8,128)(2,1)} %param.21, bf16[1,128,1024]{2,1,0:T(8,128)(2,1)} %copy-done), kind=kOutput, calls=%fused_computation.36 | convolution fusion | flops 1073741824 | bytes 10747904 | tf_op jit(solution)/shard_map/dot_general | solution.py:375
  104.2 12.5 %collective-permute-done.12.refs_0_.refs_6_ = bf16[4,128,1024]{2,1,0:T(8,128)(2,1)S(1)} collective-permute-done((bf16[4,128,1024]{2,1,0:T(8,128)(2,1)}, bf16[4,128,1024]{2,1,0:T(8,128)(2,1)S(1)}, u32[]{:S(2)}, u32[]{:S(2)}) %collective-permute-start.12) | collective-permute-done | bytes 1048608 | tf_op jit(solution)/shard_map/ppermute | solution.py:223
  116.7 3.1 %collective-permute-done.13.refs_1_.refs_7_ = bf16[4,128,1024]{2,1,0:T(8,128)(2,1)S(1)} collective-permute-done((bf16[4,128,1024]{2,1,0:T(8,128)(2,1)}, bf16[4,128,1024]{2,1,0:T(8,128)(2,1)S(1)}, u32[]{:S(2)}, u32[]{:S(2)}) %collective-permute-start.13) | collective-permute-done | bytes 1048608 | tf_op jit(solution)/shard_map/ppermute | solution.py:223
  122.3 2.2 pieces.4
  126.6 6.1 %convolution_add_fusion = f32[128,4096]{1,0:T(8,128)} fusion(f32[128,4096]{1,0:T(8,128)S(1)} %fusion.22, bf16[1024,4096]{1,0:T(8,128)(2,1)} %collective-permute-done, bf16[1,128,1024]{2,1,0:T(8,128)(2,1)S(1)} %collective-permute-done.1.refs_4_), kind=kOutput, calls=%fused_computation.1 | convolution fusion | flops 1074266112 | bytes 12845056 | tf_op jit(solution)/shard_map/dot_general | solution.py:375
  134.6 3.1 %collective-permute-done.11.refs_4_ = bf16[2,128,1024]{2,1,0:T(8,128)(2,1)} collective-permute-done((bf16[2,128,1024]{2,1,0:T(8,128)(2,1)}, bf16[2,128,1024]{2,1,0:T(8,128)(2,1)}, u32[]{:S(2)}, u32[]{:S(2)}) %collective-permute-start.11) | collective-permute-done | bytes 524320 | tf_op jit(solution)/shard_map/ppermute | solution.py:223
  137.7 4.8 %hessian_tiles.5 = f32[3,512,512]{2,1,0:T(8,128)} custom-call(s32[36]{0:T(128)S(1)} %reshape.695.where_ref, bf16[4,128,1024]{2,1,0:T(8,128)(2,1)} %get-tuple-element.55.refs_0_, bf16[4,128,1024]{2,1,0:T(8,128)(2,1)S(1)} %collective-permute-done.8.refs_0_.refs_1_, bf16[4,128,1024]{2,1,0:T(8,128)(2,1)} %collective-permute-done.9.refs_1_.refs_2_, ...), custom_call_target="tpu_custom_call" | custom-call | flops 402653184 | bytes 6291456 | tf_op jit(solution)/shard_map/hessian_tiles/pallas_call | solution.py:275
  142.5 5.4 %collective-permute-start.16 = (f32[3,512,512]{2,1,0:T(8,128)}, f32[3,512,512]{2,1,0:T(8,128)}, u32[]{:S(2)}, u32[]{:S(2)}) collective-permute-start(f32[3,512,512]{2,1,0:T(8,128)} %hessian_tiles.5), channel_id=1, source_target_pairs={{0,1},{1,0},{2,3},{3,2},{4,5},{5,4},{6,7},{7,6},{8,9},{9,8},{10,11... | collective-permute-start | bytes 9437192 | tf_op jit(solution)/shard_map/ppermute | solution.py:223
  148.2 5.0 %hessian_tiles.6 = f32[3,512,512]{2,1,0:T(8,128)} custom-call(s32[36]{0:T(128)S(1)} %reshape.696.where_ref, bf16[4,128,1024]{2,1,0:T(8,128)(2,1)} %get-tuple-element.55.refs_0_, bf16[4,128,1024]{2,1,0:T(8,128)(2,1)S(1)} %collective-permute-done.8.refs_0_.refs_1_, bf16[4,128,1024]{2,1,0:T(8,128)(2,1)} %collective-permute-done.9.refs_1_.refs_2_, ...), custom_call_target="tpu_custom_call" | custom-call | flops 402653184 | bytes 6291456 | tf_op jit(solution)/shard_map/hessian_tiles/pallas_call | solution.py:275
  158.9 3.7 %fusion.15 = (f16[512,512]{1,0:T(8,128)(2,1)}, f16[512,512]{1,0:T(8,128)(2,1)}) fusion(f32[3,512,512]{2,1,0:T(8,128)} %collective-permute-done.16, f32[3,512,512]{2,1,0:T(8,128)} %hessian_tiles.6), kind=kLoop, calls=%fused_computation.25 | loop fusion | flops 1048576 | bytes 5242880 | tf_op jit(solution)/shard_map/convert_element_type | solution.py:397
  162.6 6.9 %hessian_tiles.7 = f32[5,512,512]{2,1,0:T(8,128)} custom-call(s32[60]{0:T(128)S(1)} %reshape.697.where_ref, bf16[4,128,1024]{2,1,0:T(8,128)(2,1)} %get-tuple-element.55.refs_0_, bf16[4,128,1024]{2,1,0:T(8,128)(2,1)S(1)} %collective-permute-done.8.refs_0_.refs_1_, bf16[4,128,1024]{2,1,0:T(8,128)(2,1)} %collective-permute-done.9.refs_1_.refs_2_, ...), custom_call_target="tpu_custom_call" | custom-call | flops 671088640 | bytes 10485760 | tf_op jit(solution)/shard_map/hessian_tiles/pallas_call | solution.py:275
  170.6 2.7 %fusion.19 = (f16[512,512]{1,0:T(8,128)(2,1)}, f16[512,512]{1,0:T(8,128)(2,1)}) fusion(f16[512,512]{1,0:T(8,128)(2,1)} %get-tuple-element.74, f32[3,512,512]{2,1,0:T(8,128)} %collective-permute-done.16, f32[3,512,512]{2,1,0:T(8,128)} %hessian_tiles.6, f16[256,512]{1,0:T(8,128)(2,1)S(1)} %collective-permute-done.17, f16[512,512]{1,0:T(8,128)(2,1)} %get-tuple-element.76, ...), kind=kLoop, calls=%fused_computation.33 | loop fusion | flops 1048576 | bytes 3145728 | tf_op jit(solution)/shard_map/dynamic_update_slice | solution.py:412
  176.3 4.6 %hessian_tiles.4 = f32[5,512,512]{2,1,0:T(8,128)S(1)} custom-call(s32[60]{0:T(128)S(1)} %reshape.694.where_ref, bf16[4,128,1024]{2,1,0:T(8,128)(2,1)} %get-tuple-element.55.refs_0_, bf16[4,128,1024]{2,1,0:T(8,128)(2,1)S(1)} %collective-permute-done.8.refs_0_.refs_1_, bf16[4,128,1024]{2,1,0:T(8,128)(2,1)} %collective-permute-done.9.refs_1_.refs_2_, ...), custom_call_target="tpu_custom_call" | custom-call | flops 671088640 | bytes 10485760 | tf_op jit(solution)/shard_map/hessian_tiles/pallas_call | solution.py:275
  180.9 7.5 %collective-permute-done.20 = f16[512,512]{1,0:T(8,128)(2,1)} collective-permute-done((f16[512,512]{1,0:T(8,128)(2,1)}, f16[512,512]{1,0:T(8,128)(2,1)}, u32[]{:S(2)}, u32[]{:S(2)}) %collective-permute-start.20) | collective-permute-done | bytes 524320 | tf_op jit(solution)/shard_map/ppermute | solution.py:223
  191.9 2.7 %collective-permute-start.24 = (f16[512,512]{1,0:T(8,128)(2,1)S(1)}, f16[512,512]{1,0:T(8,128)(2,1)S(1)}, u32[]{:S(2)}, u32[]{:S(2)}) collective-permute-start(f16[512,512]{1,0:T(8,128)(2,1)S(1)} %fusion.13), channel_id=1, source_target_pairs={{0,112},{16,0},{32,16},{48,32},{64,48},{80,64},{96,80},{112,96},{1... | collective-permute-start | bytes 1572872 | tf_op jit(solution)/shard_map/ppermute | solution.py:223
  194.6 9.4 %collective-permute-done.21 = f16[512,512]{1,0:T(8,128)(2,1)S(1)} collective-permute-done((f16[512,512]{1,0:T(8,128)(2,1)S(1)}, f16[512,512]{1,0:T(8,128)(2,1)S(1)}, u32[]{:S(2)}, u32[]{:S(2)}) %collective-permute-start.21) | collective-permute-done | bytes 524320 | tf_op jit(solution)/shard_map/ppermute | solution.py:223
  207.2 2.7 %collective-permute-start.25 = (f16[512,512]{1,0:T(8,128)(2,1)S(1)}, f16[512,512]{1,0:T(8,128)(2,1)S(1)}, u32[]{:S(2)}, u32[]{:S(2)}) collective-permute-start(f16[512,512]{1,0:T(8,128)(2,1)S(1)} %fusion.12), channel_id=1, source_target_pairs={{0,112},{16,0},{32,16},{48,32},{64,48},{80,64},{96,80},{112,96},{1... | collective-permute-start | bytes 1572872 | tf_op jit(solution)/shard_map/ppermute | solution.py:223
  210.0 8.7 %collective-permute-done.22 = f16[512,512]{1,0:T(8,128)(2,1)S(1)} collective-permute-done((f16[512,512]{1,0:T(8,128)(2,1)S(1)}, f16[512,512]{1,0:T(8,128)(2,1)S(1)}, u32[]{:S(2)}, u32[]{:S(2)}) %collective-permute-start.22) | collective-permute-done | bytes 524320 | tf_op jit(solution)/shard_map/ppermute | solution.py:223
  219.2 2.6 %fusion.10 = f32[1,512,512]{2,1,0:T(8,128)} fusion(f32[5,512,512]{2,1,0:T(8,128)} %collective-permute-done.19, f32[5,512,512]{2,1,0:T(8,128)S(1)} %hessian_tiles.4, f16[512,512]{1,0:T(8,128)(2,1)S(1)} %collective-permute-done.25, f16[512,512]{1,0:T(8,128)(2,1)S(1)} %collective-permute-done.22), kind=kLoop, calls=%fused_computation.15 | loop fusion | flops 1572864 | bytes 4194304 | tf_op jit(solution)/shard_map/broadcast_in_dim | solution.py:420
  (115 shorter events, 44.2 us)
Async XLA Ops:
  7.2 38.2 %copy-start.2 = (f32[16,64,256]{2,1,0:T(8,128)S(1)}, f32[16,64,256]{2,1,0:T(8,128)}, u32[]{:S(2)}) copy-start(f32[16,64,256]{2,1,0:T(8,128)} %param.19) | copy-start | bytes 3145732
  7.2 38.1 %collective-permute-start = (bf16[1024,4096]{1,0:T(8,128)(2,1)}, bf16[1024,4096]{1,0:T(8,128)(2,1)}, u32[]{:S(2)}, u32[]{:S(2)}) collective-permute-start(bf16[1024,4096]{1,0:T(8,128)(2,1)} %param.21), channel_id=1, source_target_pairs={{0,1},{1,0},{2,3},{3,2},{4,5},{5,4},{6,7},{7,6},{8,9},{9,8},{10,11... | collective-permute-start | bytes 25165832 | tf_op jit(solution)/shard_map/ppermute | solution.py:223
  17.2 36.6 %copy-start.1 = (bf16[256,2048]{1,0:T(8,128)(2,1)S(1)}, bf16[256,2048]{1,0:T(8,128)(2,1)}, u32[]{:S(2)}) copy-start(bf16[256,2048]{1,0:T(8,128)(2,1)} %c_ref.3) | copy-start | bytes 3145732
  17.2 36.6 %copy-start.4 = (bf16[256,2048]{1,0:T(8,128)(2,1)S(1)}, bf16[256,2048]{1,0:T(8,128)(2,1)}, u32[]{:S(2)}) copy-start(bf16[256,2048]{1,0:T(8,128)(2,1)} %b_ref.3) | copy-start | bytes 3145732
  17.2 36.6 %copy-start.9 = (f32[256,16]{0,1:T(8,128)S(1)}, f32[256,16]{0,1:T(8,128)}, u32[]{:S(2)}) copy-start(f32[256,16]{0,1:T(8,128)} %param.16) | copy-start | bytes 49156
  48.3 19.1 %all-to-all-start.1 = ((f16[16,136,128]{2,1,0:T(8,128)(2,1)}), f16[16,136,128]{2,1,0:T(8,128)(2,1)}, u32[]{:S(2)}, u32[]{:S(2)}) async-start(f16[16,136,128]{2,1,0:T(8,128)(2,1)} %convert_element_type.112), calls=%async_computation.1 | async-start | bytes 1114112 | tf_op jit(solution)/shard_map/all_to_all | solution.py:334
  52.6 169.2 %reduce-scatter.2.cloned.1.call-start = ((), (), s32[]{:S(2)}) async-start(), calls=%async_computation.3 | async-start | bytes 2359296 | tf_op jit(solution)/shard_map/reduce_scatter | solution.py:379
  72.0 6.1 %collective-permute-start.1 = (bf16[1,128,1024]{2,1,0:T(8,128)(2,1)S(1)}, bf16[1,128,1024]{2,1,0:T(8,128)(2,1)S(1)}, u32[]{:S(2)}, u32[]{:S(2)}) collective-permute-start(bf16[1,128,1024]{2,1,0:T(8,128)(2,1)S(1)} %get-tuple-element.46), channel_id=1, source_target_pairs={{0,1},{1,0},{2,3},{3,2},{4,5},{5,4},{6,7},{7,6},{8,9},{9,8},{10,11... | collective-permute-start | bytes 786440 | tf_op jit(solution)/shard_map/ppermute | solution.py:223
  75.5 7.9 %collective-permute-start.2 = (bf16[1,128,1024]{2,1,0:T(8,128)(2,1)S(1)}, bf16[1,128,1024]{2,1,0:T(8,128)(2,1)S(1)}, u32[]{:S(2)}, u32[]{:S(2)}) collective-permute-start(bf16[1,128,1024]{2,1,0:T(8,128)(2,1)S(1)} %get-tuple-element.45.refs_0_), channel_id=1, source_target_pairs={{0,130},{2,0},{128,2},{130,128},{1,131},{3,1},{129,3},{131,129},{4... | collective-permute-start | bytes 786440 | tf_op jit(solution)/shard_map/ppermute | solution.py:223
  76.3 14.4 %collective-permute-start.3 = (bf16[1,128,1024]{2,1,0:T(8,128)(2,1)S(1)}, bf16[1,128,1024]{2,1,0:T(8,128)(2,1)S(1)}, u32[]{:S(2)}, u32[]{:S(2)}) collective-permute-start(bf16[1,128,1024]{2,1,0:T(8,128)(2,1)S(1)} %get-tuple-element.45.refs_0_), channel_id=1, source_target_pairs={{0,2},{2,128},{128,130},{130,0},{1,3},{3,129},{129,131},{131,1},{4... | collective-permute-start | bytes 786440 | tf_op jit(solution)/shard_map/ppermute | solution.py:223
  77.1 13.7 %collective-permute-start.4 = (bf16[1,128,1024]{2,1,0:T(8,128)(2,1)S(1)}, bf16[1,128,1024]{2,1,0:T(8,128)(2,1)S(1)}, u32[]{:S(2)}, u32[]{:S(2)}) collective-permute-start(bf16[1,128,1024]{2,1,0:T(8,128)(2,1)S(1)} %get-tuple-element.45.refs_0_), channel_id=1, source_target_pairs={{0,128},{2,130},{128,0},{130,2},{1,129},{3,131},{129,1},{131,3},{4... | collective-permute-start | bytes 786440 | tf_op jit(solution)/shard_map/ppermute | solution.py:223
  78.1 12.7 %collective-permute-start.5 = (bf16[1,128,1024]{2,1,0:T(8,128)(2,1)S(1)}, bf16[1,128,1024]{2,1,0:T(8,128)(2,1)S(1)}, u32[]{:S(2)}, u32[]{:S(2)}) collective-permute-start(bf16[1,128,1024]{2,1,0:T(8,128)(2,1)S(1)} %collective-permute-done.1.refs_4_), channel_id=1, source_target_pairs={{0,12},{4,0},{8,4},{12,8},{1,13},{5,1},{9,5},{13,9},{2,14},{6,2},{... | collective-permute-start | bytes 786440 | tf_op jit(solution)/shard_map/ppermute | solution.py:223
  80.8 9.9 %collective-permute-start.6 = (bf16[1,128,1024]{2,1,0:T(8,128)(2,1)S(1)}, bf16[1,128,1024]{2,1,0:T(8,128)(2,1)S(1)}, u32[]{:S(2)}, u32[]{:S(2)}) collective-permute-start(bf16[1,128,1024]{2,1,0:T(8,128)(2,1)S(1)} %collective-permute-done.1.refs_4_), channel_id=1, source_target_pairs={{0,4},{4,8},{8,12},{12,0},{1,5},{5,9},{9,13},{13,1},{2,6},{6,10},{... | collective-permute-start | bytes 786440 | tf_op jit(solution)/shard_map/ppermute | solution.py:223
  83.3 9.9 %collective-permute-start.7 = (bf16[1,128,1024]{2,1,0:T(8,128)(2,1)S(1)}, bf16[1,128,1024]{2,1,0:T(8,128)(2,1)S(1)}, u32[]{:S(2)}, u32[]{:S(2)}) collective-permute-start(bf16[1,128,1024]{2,1,0:T(8,128)(2,1)S(1)} %collective-permute-done.1.refs_4_), channel_id=1, source_target_pairs={{0,8},{4,12},{8,0},{12,4},{1,9},{5,13},{9,1},{13,5},{2,10},{6,14},... | collective-permute-start | bytes 786440 | tf_op jit(solution)/shard_map/ppermute | solution.py:223
  94.8 22.0 %collective-permute-start.12 = (bf16[4,128,1024]{2,1,0:T(8,128)(2,1)}, bf16[4,128,1024]{2,1,0:T(8,128)(2,1)S(1)}, u32[]{:S(2)}, u32[]{:S(2)}) collective-permute-start(bf16[4,128,1024]{2,1,0:T(8,128)(2,1)} %get-tuple-element.60.refs_5_), channel_id=1, source_target_pairs={{0,130},{2,0},{128,2},{130,128},{1,131},{3,1},{129,3},{131,129},{4... | collective-permute-start | bytes 3145736 | tf_op jit(solution)/shard_map/ppermute | solution.py:223
  96.7 23.1 %collective-permute-start.13 = (bf16[4,128,1024]{2,1,0:T(8,128)(2,1)}, bf16[4,128,1024]{2,1,0:T(8,128)(2,1)S(1)}, u32[]{:S(2)}, u32[]{:S(2)}) collective-permute-start(bf16[4,128,1024]{2,1,0:T(8,128)(2,1)} %get-tuple-element.60.refs_5_), channel_id=1, source_target_pairs={{0,2},{2,128},{128,130},{130,0},{1,3},{3,129},{129,131},{131,1},{4... | collective-permute-start | bytes 3145736 | tf_op jit(solution)/shard_map/ppermute | solution.py:223
  96.7 25.6 %collective-permute-start.8 = (bf16[4,128,1024]{2,1,0:T(8,128)(2,1)}, bf16[4,128,1024]{2,1,0:T(8,128)(2,1)S(1)}, u32[]{:S(2)}, u32[]{:S(2)}) collective-permute-start(bf16[4,128,1024]{2,1,0:T(8,128)(2,1)} %get-tuple-element.55.refs_0_), channel_id=1, source_target_pairs={{0,12},{4,0},{8,4},{12,8},{1,13},{5,1},{9,5},{13,9},{2,14},{6,2},{... | collective-permute-start | bytes 3145736 | tf_op jit(solution)/shard_map/ppermute | solution.py:223
  97.9 24.4 %collective-permute-start.9 = (bf16[4,128,1024]{2,1,0:T(8,128)(2,1)}, bf16[4,128,1024]{2,1,0:T(8,128)(2,1)}, u32[]{:S(2)}, u32[]{:S(2)}) collective-permute-start(bf16[4,128,1024]{2,1,0:T(8,128)(2,1)} %get-tuple-element.55.refs_0_), channel_id=1, source_target_pairs={{0,4},{4,8},{8,12},{12,0},{1,5},{5,9},{9,13},{13,1},{2,6},{6,10},{... | collective-permute-start | bytes 3145736 | tf_op jit(solution)/shard_map/ppermute | solution.py:223
  120.9 11.9 %collective-permute-start.14 = (bf16[2,128,1024]{2,1,0:T(8,128)(2,1)}, bf16[2,128,1024]{2,1,0:T(8,128)(2,1)}, u32[]{:S(2)}, u32[]{:S(2)}) collective-permute-start(bf16[2,128,1024]{2,1,0:T(8,128)(2,1)} %get-tuple-element.52), channel_id=1, source_target_pairs={{0,130},{2,0},{128,2},{130,128},{1,131},{3,1},{129,3},{131,129},{4... | collective-permute-start | bytes 1572872 | tf_op jit(solution)/shard_map/ppermute | solution.py:223
  121.2 11.6 %collective-permute-start.15 = (bf16[2,128,1024]{2,1,0:T(8,128)(2,1)}, bf16[2,128,1024]{2,1,0:T(8,128)(2,1)}, u32[]{:S(2)}, u32[]{:S(2)}) collective-permute-start(bf16[2,128,1024]{2,1,0:T(8,128)(2,1)} %get-tuple-element.53), channel_id=1, source_target_pairs={{0,2},{2,128},{128,130},{130,0},{1,3},{3,129},{129,131},{131,1},{4... | collective-permute-start | bytes 1572872 | tf_op jit(solution)/shard_map/ppermute | solution.py:223
  124.6 10.0 %collective-permute-start.10 = (bf16[2,128,1024]{2,1,0:T(8,128)(2,1)}, bf16[2,128,1024]{2,1,0:T(8,128)(2,1)}, u32[]{:S(2)}, u32[]{:S(2)}) collective-permute-start(bf16[2,128,1024]{2,1,0:T(8,128)(2,1)} %get-tuple-element.49), channel_id=1, source_target_pairs={{0,12},{4,0},{8,4},{12,8},{1,13},{5,1},{9,5},{13,9},{2,14},{6,2},{... | collective-permute-start | bytes 1572872 | tf_op jit(solution)/shard_map/ppermute | solution.py:223
  126.6 11.1 %collective-permute-start.11 = (bf16[2,128,1024]{2,1,0:T(8,128)(2,1)}, bf16[2,128,1024]{2,1,0:T(8,128)(2,1)}, u32[]{:S(2)}, u32[]{:S(2)}) collective-permute-start(bf16[2,128,1024]{2,1,0:T(8,128)(2,1)} %get-tuple-element.50), channel_id=1, source_target_pairs={{0,4},{4,8},{8,12},{12,0},{1,5},{5,9},{9,13},{13,1},{2,6},{6,10},{... | collective-permute-start | bytes 1572872 | tf_op jit(solution)/shard_map/ppermute | solution.py:223
  142.5 11.0 %collective-permute-start.16 = (f32[3,512,512]{2,1,0:T(8,128)}, f32[3,512,512]{2,1,0:T(8,128)}, u32[]{:S(2)}, u32[]{:S(2)}) collective-permute-start(f32[3,512,512]{2,1,0:T(8,128)} %hessian_tiles.5), channel_id=1, source_target_pairs={{0,1},{1,0},{2,3},{3,2},{4,5},{5,4},{6,7},{7,6},{8,9},{9,8},{10,11... | collective-permute-start | bytes 9437192 | tf_op jit(solution)/shard_map/ppermute | solution.py:223
  156.2 13.3 %collective-permute-start.17 = (f16[256,512]{1,0:T(8,128)(2,1)}, f16[256,512]{1,0:T(8,128)(2,1)S(1)}, u32[]{:S(2)}, u32[]{:S(2)}) collective-permute-start(f16[256,512]{1,0:T(8,128)(2,1)} %get-tuple-element.91), channel_id=1, source_target_pairs={{0,16},{16,32},{32,48},{48,64},{64,80},{80,96},{96,112},{112,0},{1... | collective-permute-start | bytes 786440 | tf_op jit(solution)/shard_map/ppermute | solution.py:223
  157.5 12.0 %collective-permute-start.18 = (f16[256,512]{1,0:T(8,128)(2,1)}, f16[256,512]{1,0:T(8,128)(2,1)}, u32[]{:S(2)}, u32[]{:S(2)}) collective-permute-start(f16[256,512]{1,0:T(8,128)(2,1)} %get-tuple-element.90), channel_id=1, source_target_pairs={{0,112},{16,0},{32,16},{48,32},{64,48},{80,64},{96,80},{112,96},{1... | collective-permute-start | bytes 786440 | tf_op jit(solution)/shard_map/ppermute | solution.py:223
  169.5 18.9 %collective-permute-start.19 = (f32[5,512,512]{2,1,0:T(8,128)}, f32[5,512,512]{2,1,0:T(8,128)}, u32[]{:S(2)}, u32[]{:S(2)}) collective-permute-start(f32[5,512,512]{2,1,0:T(8,128)} %hessian_tiles.7), channel_id=1, source_target_pairs={{0,1},{1,0},{2,3},{3,2},{4,5},{5,4},{6,7},{7,6},{8,9},{9,8},{10,11... | collective-permute-start | bytes 15728648 | tf_op jit(solution)/shard_map/ppermute | solution.py:223
  173.3 15.1 %collective-permute-start.20 = (f16[512,512]{1,0:T(8,128)(2,1)}, f16[512,512]{1,0:T(8,128)(2,1)}, u32[]{:S(2)}, u32[]{:S(2)}) collective-permute-start(f16[512,512]{1,0:T(8,128)(2,1)} %get-tuple-element.86), channel_id=1, source_target_pairs={{0,16},{16,32},{32,48},{48,64},{64,80},{80,96},{96,112},{112,0},{1... | collective-permute-start | bytes 1572872 | tf_op jit(solution)/shard_map/ppermute | solution.py:223
  173.8 16.4 %collective-permute-start.23 = (f16[512,512]{1,0:T(8,128)(2,1)}, f16[512,512]{1,0:T(8,128)(2,1)}, u32[]{:S(2)}, u32[]{:S(2)}) collective-permute-start(f16[512,512]{1,0:T(8,128)(2,1)} %get-tuple-element.87), channel_id=1, source_target_pairs={{0,112},{16,0},{32,16},{48,32},{64,48},{80,64},{96,80},{112,96},{1... | collective-permute-start | bytes 1572872 | tf_op jit(solution)/shard_map/ppermute | solution.py:223
  190.1 13.9 %collective-permute-start.21 = (f16[512,512]{1,0:T(8,128)(2,1)S(1)}, f16[512,512]{1,0:T(8,128)(2,1)S(1)}, u32[]{:S(2)}, u32[]{:S(2)}) collective-permute-start(f16[512,512]{1,0:T(8,128)(2,1)S(1)} %fusion.5), channel_id=1, source_target_pairs={{0,16},{16,32},{32,48},{48,64},{64,80},{80,96},{96,112},{112,0},{1... | collective-permute-start | bytes 1572872 | tf_op jit(solution)/shard_map/ppermute | solution.py:223
  191.9 13.8 %collective-permute-start.24 = (f16[512,512]{1,0:T(8,128)(2,1)S(1)}, f16[512,512]{1,0:T(8,128)(2,1)S(1)}, u32[]{:S(2)}, u32[]{:S(2)}) collective-permute-start(f16[512,512]{1,0:T(8,128)(2,1)S(1)} %fusion.13), channel_id=1, source_target_pairs={{0,112},{16,0},{32,16},{48,32},{64,48},{80,64},{96,80},{112,96},{1... | collective-permute-start | bytes 1572872 | tf_op jit(solution)/shard_map/ppermute | solution.py:223
  205.6 13.1 %collective-permute-start.22 = (f16[512,512]{1,0:T(8,128)(2,1)S(1)}, f16[512,512]{1,0:T(8,128)(2,1)S(1)}, u32[]{:S(2)}, u32[]{:S(2)}) collective-permute-start(f16[512,512]{1,0:T(8,128)(2,1)S(1)} %fusion.2), channel_id=1, source_target_pairs={{0,16},{16,32},{32,48},{48,64},{64,80},{80,96},{96,112},{112,0},{1... | collective-permute-start | bytes 1572872 | tf_op jit(solution)/shard_map/ppermute | solution.py:223
  207.2 12.0 %collective-permute-start.25 = (f16[512,512]{1,0:T(8,128)(2,1)S(1)}, f16[512,512]{1,0:T(8,128)(2,1)S(1)}, u32[]{:S(2)}, u32[]{:S(2)}) collective-permute-start(f16[512,512]{1,0:T(8,128)(2,1)S(1)} %fusion.12), channel_id=1, source_target_pairs={{0,112},{16,0},{32,16},{48,32},{64,48},{80,64},{96,80},{112,96},{1... | collective-permute-start | bytes 1572872 | tf_op jit(solution)/shard_map/ppermute | solution.py:223
  (11 other events, 159.7 us)
Sparse Core Ops, SparseCore 0:
  170.7 48.8 reduce-scatter.1
